TPU v7x, 128 devices: a whole 4x4x4 slice. The times are simulated.
128 devices in a mesh: sub: 16 (over y, x), grp: 8 (over z, core).
Axes of the slice: x: 4, y: 4, z: 4, core: 2. Of those that a mesh axis runs over, the one named last changes fastest.
Arguments:
- schur: bfloat16 [128, 2560, 2560], P(('sub', 'grp'))
- coarse_basis: float32 [128, 6, 2560], P(('sub', 'grp')), may hold values from -0.125 to 0.125
- coarse_inverse: float32 [768, 768], P(('sub', 'grp'))
- coarse_coeff: float32 [128, 6, 96], P(('sub', 'grp')), may hold values from -160 to 160
- dual_load: float32 [128, 96, 2560], P(('sub', 'grp'))
- face_order: int32 [128, 2, 512], P(('sub', 'grp')), may hold values from 0 to 511, each once within a row
- contact_partner: int32 [128, 256], P(('sub', 'grp')), may hold values from 0 to 255, as said below
- active_flags: int32 [128, 96, 256], P(('sub', 'grp')), may hold values from 0 to 1, as said below
- step_codes: int32 [96, 3], replicated, may hold values from 0 to 2
Outputs:
- multipliers: float32 [128, 96, 2560], P(('sub', 'grp'))
- gradient: float32 [128, 96, 2560], P(('sub', 'grp'))
Inputs may be any that keep to these rules, and one draw needn't show every extreme that they name: `contact_partner`: the subdomains at (i, j) and (i, j + 4) hold mutually inverse maps. `active_flags`: the two multipliers of a contact pair carry the same flag.
All inputs are finite; a program needn't handle non-finite values.
Results may differ from a plain program's by a relative error of at most 0.0035.
Values sent between devices are 32-bit elements; how exact they have to be, the bound alone decides.
No kernel may reach another device: no remote copies, remote signals or barrier semaphores. Data moves between devices by JAX's collectives and lax.ppermute only.
A program may use at most 128 MiB of HBM per device.

v0:
```python
import jax
import jax.numpy as jnp
from jax import lax
from jax.sharding import PartitionSpec as P

FACE = 512
CONT = 256
DIRI = 256
MODES = 6
ITERS = 3


highest = lax.Precision.HIGHEST
step_scale = 0.2


def extended(block, sides, width):
    for axis, dim in sides:
        count = lax.axis_size(axis)
        forward = [(i, i + 1) for i in range(count - 1)]
        backward = [(target, source) for source, target in forward]
        low = lax.ppermute(
            lax.slice_in_dim(block, block.shape[dim] - width, None, axis=dim), axis, forward
        )
        high = lax.ppermute(lax.slice_in_dim(block, 0, width, axis=dim), axis, backward)
        block = jnp.concatenate([low, block, high], axis=dim)
    return block


def swapped(block, axis, distance):
    count = lax.axis_size(axis)
    route = []
    for low in range(count):
        high = low | 1 << distance
        if high != low and high < count:
            route += [(low, high), (high, low)]
    return lax.ppermute(block, axis, route)


def shards(
    schur,
    coarse_basis,
    coarse_inverse,
    coarse_coeff,
    dual_load,
    face_order,
    contact_partner,
    active_flags,
    step_codes,
):
    schur_block = schur[0]
    basis_rows = coarse_basis[0]
    sub_index = lax.axis_index("sub")
    group_index = lax.axis_index("grp")
    sub_count = lax.axis_size("sub")
    group_count = lax.axis_size("grp")
    quarter = group_count // 4
    top_bit = group_count.bit_length() - 2
    domain_count = sub_count * group_count
    domain_rank = sub_index * group_count + group_index
    lower_flag = (sub_index > 0).astype(jnp.float32)
    upper_flag = (sub_index < sub_count - 1).astype(jnp.float32)
    keep_lower = ((group_index != quarter) & (group_index != 3 * quarter)).astype(jnp.float32)
    keep_upper = ((group_index != quarter - 1) & (group_index != 3 * quarter - 1)).astype(
        jnp.float32
    )
    group_lower_flag = keep_lower * (group_index > 0).astype(jnp.float32)
    group_upper_flag = keep_upper * (group_index < group_count - 1).astype(jnp.float32)
    face_ones = jnp.ones((FACE,), jnp.float32)
    multiplicity = jnp.concatenate(
        [
            face_ones + lower_flag,
            face_ones + upper_flag,
            face_ones + group_lower_flag,
            face_ones + group_upper_flag,
            jnp.full((CONT,), 2.0, jnp.float32),
            jnp.ones((DIRI,), jnp.float32),
        ]
    )
    weight = 1.0 / multiplicity
    sub_order = face_order[0, 0]
    group_order = face_order[0, 1]
    sub_inverse = jnp.argsort(sub_order)
    group_inverse = jnp.argsort(group_order)
    partner_map = contact_partner[0]
    load_count = dual_load.shape[1]

    def received(local_part):
        lower_face = local_part[:, :FACE]
        upper_face = local_part[:, FACE : 2 * FACE]
        group_lower = local_part[:, 2 * FACE : 3 * FACE]
        group_upper = local_part[:, 3 * FACE : 4 * FACE]
        contact_part = local_part[:, 4 * FACE : 4 * FACE + CONT]
        sub_stack = jnp.stack([lower_face, jnp.take(upper_face, sub_inverse, axis=1)])
        padded = extended(sub_stack, (("sub", 0),), 1)
        from_lower = padded[0]
        from_upper = jnp.take(padded[3], sub_order, axis=1)
        group_stack = jnp.stack([group_lower, jnp.take(group_upper, group_inverse, axis=1)])
        group_padded = extended(group_stack, (("grp", 0),), 1)
        from_group_lower = group_padded[0] * keep_lower
        from_group_upper = jnp.take(group_padded[3], group_order, axis=1) * keep_upper
        partner_part = swapped(contact_part, "grp", top_bit)
        from_contact = jnp.take(partner_part, partner_map, axis=1)
        dirichlet = jnp.zeros((local_part.shape[0], DIRI), jnp.float32)
        return jnp.concatenate(
            [from_lower, from_upper, from_group_lower, from_group_upper, from_contact, dirichlet],
            axis=1,
        )

    def assemble(local_part):
        return local_part + received(local_part)

    def collect(piece_stack, target_ranks):
        domain_ids = jnp.arange(domain_count, dtype=jnp.int32)
        matched = (domain_ids == target_ranks[0])[:, None, None]
        placed = jnp.where(matched, piece_stack[0][None], 0.0)
        return lax.psum(placed, ("sub", "grp")).reshape(domain_count * MODES, load_count)

    def coarse_apply(coef_all):
        alpha_coef = jnp.dot(coarse_inverse, coef_all, precision=highest)
        return jnp.einsum("ml,mo->lo", alpha_coef, basis_rows, precision=highest)

    def project(field_vec):
        own_coef = jnp.einsum("lo,mo->ml", field_vec, basis_rows, precision=highest)
        return field_vec - assemble(coarse_apply(collect(own_coef[None], [domain_rank])))

    def project_assembled(local_part):
        return project(assemble(local_part))

    def operator(field_vec):
        rounded = project(field_vec).astype(jnp.bfloat16)
        product = jnp.dot(rounded, schur_block, preferred_element_type=jnp.float32)
        return project_assembled(product)

    def inner_sum(left, right):
        return jnp.sum(left * right * weight[None, :], axis=1)

    flag_rows = active_flags[0].astype(jnp.float32)
    active = jnp.concatenate(
        [
            jnp.zeros((load_count, 4 * FACE), jnp.float32),
            flag_rows,
            jnp.zeros((load_count, DIRI), jnp.float32),
        ],
        axis=1,
    )
    free_mask = 1.0 - active
    contact_mask = jnp.concatenate(
        [
            jnp.zeros((4 * FACE,), jnp.float32),
            jnp.ones((CONT,), jnp.float32),
            jnp.zeros((DIRI,), jnp.float32),
        ]
    )
    start_point = assemble(jnp.einsum("ml,mo->lo", coarse_coeff[0], basis_rows, precision=highest))
    multipliers = jnp.where(contact_mask > 0, jnp.maximum(start_point, 0.0), start_point)
    load_vec = project_assembled(dual_load[0])
    gradient = operator(multipliers) - load_vec
    direction = free_mask * gradient
    for step_number in range(ITERS):
        step_code = step_codes[:, step_number]
        code_wide = step_code[:, None]
        free_grad = free_mask * gradient
        chopped = active * jnp.minimum(gradient, 0.0)
        trial_point = multipliers - step_scale * free_grad
        trial_point = jnp.where(contact_mask > 0, jnp.maximum(trial_point, 0.0), trial_point)
        search = jnp.where(
            code_wide == 0, direction, jnp.where(code_wide == 2, chopped, trial_point - multipliers)
        )
        image_vec = operator(search)
        slope_sum, curve_sum, cross_sum, bend_sum = lax.psum(
            (
                inner_sum(gradient, search),
                inner_sum(search, image_vec),
                inner_sum(free_grad, image_vec),
                inner_sum(free_mask * image_vec, image_vec),
            ),
            ("sub", "grp"),
        )
        length = jnp.where(step_code == 1, -1.0, slope_sum / curve_sum)
        conj_factor = jnp.where(step_code == 0, (cross_sum - length * bend_sum) / curve_sum, 0.0)
        multipliers = multipliers - length[:, None] * search
        gradient = gradient - length[:, None] * image_vec
        direction = free_mask * gradient - conj_factor[:, None] * direction
    return (multipliers[None], gradient[None])


def solution(mesh):
    in_specs = (
        P(("sub", "grp"), None, None),
        P(("sub", "grp"), None, None),
        P(("sub", "grp"), None),
        P(("sub", "grp"), None, None),
        P(("sub", "grp"), None, None),
        P(("sub", "grp"), None, None),
        P(("sub", "grp"), None),
        P(("sub", "grp"), None, None),
        P(),
    )
    out_specs = (P(("sub", "grp"), None, None), P(("sub", "grp"), None, None))
    return jax.shard_map(shards, mesh=mesh, in_specs=in_specs, out_specs=out_specs, check_vma=False)
```

profile of v0, /device:TPU:1, one launch (start us, length us, event | category | flops | bytes accessed | tf_op | source)
XLA Modules:
  0.0 2006.4 jit_solution(6691909553270824857)
XLA Ops:
  8.0 3.8 sort.31
  11.8 3.8 sort.32
  18.8 4.6 collective-permute-start
  26.8 4.4 collective-permute-start.2
  33.1 3.4 collective-permute-start.4
  67.3 136.2 %all-reduce.13.cloned.1.call-done = f32[768,96]{1,0:T(8,128)} async-done(((f32[768,96]{1,0:T(8,128)}), f32[768,96]{1,0:T(8,128)}) %all-reduce.13.cloned.1.call-update) | async-done | bytes 294928 | tf_op jit(solution)/shard_map/psum | solution.py:117
  213.4 3.7 collective-permute-start.8
  218.9 3.5 collective-permute-start.7
  230.6 7.0 fusion.6
  244.7 5.0 collective-permute-start.20
  255.7 4.9 collective-permute-start.22
  298.1 146.8 %all-reduce.27.cloned.1.call-done = (f32[768,96]{1,0:T(8,128)}, f32[768,96]{1,0:T(8,128)}) async-done(((f32[768,96]{1,0:T(8,128)}, f32[768,96]{1,0:T(8,128)}), (f32[768,96]{1,0:T(8,128)}, f32[768,96]{1,0:T(8,128)})) %all-reduce.27.cloned.1.call-update) | async-done | bytes 589840 | tf_op jit(solution)/shard_map/psum | solution.py:117
  471.6 4.2 collective-permute-start.18
  482.8 3.6 collective-permute-start.27
  487.8 5.6 collective-permute-start.25
  521.9 142.0 %all-reduce.15.cloned.1.call-done = f32[768,96]{1,0:T(8,128)} async-done(((f32[768,96]{1,0:T(8,128)}), f32[768,96]{1,0:T(8,128)}) %all-reduce.15.cloned.1.call-update) | async-done | bytes 294928 | tf_op jit(solution)/shard_map/psum | solution.py:117
  680.3 3.7 collective-permute-start.33
  685.8 3.7 collective-permute-start.32
  704.9 7.3 fusion.4
  718.3 4.9 collective-permute-start.35
  732.8 3.7 collective-permute-start.37
  758.7 146.8 %all-reduce.17.cloned.1.call-done = f32[768,96]{1,0:T(8,128)} async-done(((f32[768,96]{1,0:T(8,128)}), f32[768,96]{1,0:T(8,128)}) %all-reduce.17.cloned.1.call-update) | async-done | bytes 294928 | tf_op jit(solution)/shard_map/psum | solution.py:117
  922.0 3.7 collective-permute-start.43
  927.5 3.3 collective-permute-start.42
  946.8 3.3 fusion.12
  950.1 67.0 %all-reduce.2 = (f32[96]{0:T(128)S(1)}, f32[96]{0:T(128)S(1)}, f32[96]{0:T(128)S(1)}, f32[96]{0:T(128)S(1)}) all-reduce(f32[96]{0:T(128)S(1)} %get-tuple-element.12, f32[96]{0:T(128)S(1)} %get-tuple-element.13, f32[96]{0:T(128)S(1)} %get-tuple-element.11, f32[96]{0:T(128)S(1)} %get-tuple-element.10), channel_id=1, replica_groups=mesh['sub'=16,'grp'=8] {'sub','grp'}, use_global_device_ids=true, to_apply=%region_6.9 | all-reduce | flops 384 | bytes 3072 | tf_op jit(solution)/shard_map/psum | solution.py:171
  1025.3 141.8 %all-reduce.19.cloned.1.call-done = f32[768,96]{1,0:T(8,128)} async-done(((f32[768,96]{1,0:T(8,128)}), f32[768,96]{1,0:T(8,128)}) %all-reduce.19.cloned.1.call-update) | async-done | bytes 294928 | tf_op jit(solution)/shard_map/psum | solution.py:117
  1183.7 3.7 collective-permute-start.48
  1189.1 3.3 collective-permute-start.47
  1208.4 7.3 fusion.2
  1221.9 4.9 collective-permute-start.50
  1236.3 3.9 collective-permute-start.52
  1262.3 147.5 %all-reduce.21.cloned.1.call-done = f32[768,96]{1,0:T(8,128)} async-done(((f32[768,96]{1,0:T(8,128)}), f32[768,96]{1,0:T(8,128)}) %all-reduce.21.cloned.1.call-update) | async-done | bytes 294928 | tf_op jit(solution)/shard_map/psum | solution.py:117
  1426.3 3.7 collective-permute-start.58
  1451.1 3.6 fusion.17
  1454.7 66.8 %all-reduce.1 = (f32[96]{0:T(128)S(1)}, f32[96]{0:T(128)S(1)}, f32[96]{0:T(128)S(1)}, f32[96]{0:T(128)S(1)}) all-reduce(f32[96]{0:T(128)S(1)} %get-tuple-element.14, f32[96]{0:T(128)S(1)} %get-tuple-element.15, f32[96]{0:T(128)S(1)} %get-tuple-element.9, f32[96]{0:T(128)S(1)} %get-tuple-element.8), channel_id=1, replica_groups=mesh['sub'=16,'grp'=8] {'sub','grp'}, use_global_device_ids=true, to_apply=%region_16.19 | all-reduce | flops 384 | bytes 3072 | tf_op jit(solution)/shard_map/psum | solution.py:171
  1522.2 3.8 fusion.20
  1529.6 141.9 %all-reduce.23.cloned.1.call-done = f32[768,96]{1,0:T(8,128)} async-done(((f32[768,96]{1,0:T(8,128)}), f32[768,96]{1,0:T(8,128)}) %all-reduce.23.cloned.1.call-update) | async-done | bytes 294928 | tf_op jit(solution)/shard_map/psum | solution.py:117
  1681.6 3.7 collective-permute-start.63
  1687.1 3.3 collective-permute-start.62
  1698.1 7.0 fusion
  1708.0 4.9 collective-permute-start.65
  1720.0 3.7 collective-permute-start.67
  1739.0 147.6 %all-reduce.25.cloned.1.call-done = f32[768,96]{1,0:T(8,128)} async-done(((f32[768,96]{1,0:T(8,128)}), f32[768,96]{1,0:T(8,128)}) %all-reduce.25.cloned.1.call-update) | async-done | bytes 294928 | tf_op jit(solution)/shard_map/psum | solution.py:117
  1902.4 3.7 collective-permute-start.73
  1907.9 3.6 collective-permute-start.72
  1927.5 66.8 %all-reduce = (f32[96]{0:T(128)S(1)}, f32[96]{0:T(128)S(1)}) all-reduce(f32[96]{0:T(128)S(1)} %get-tuple-element.17, f32[96]{0:T(128)S(1)} %get-tuple-element.16), channel_id=1, replica_groups=mesh['sub'=16,'grp'=8] {'sub','grp'}, use_global_device_ids=true, to_apply=%region_26.29 | all-reduce | flops 192 | bytes 1536 | tf_op jit(solution)/shard_map/psum | solution.py:171
  1995.0 4.1 subtract_bitcast_fusion
  (679 shorter events, 478.0 us)
Async XLA Ops:
  7.2 196.2 %all-reduce.13.cloned.1.call-start = ((), (), s32[]{:S(2)}) async-start(), calls=%async_computation | async-start | bytes 786432 | tf_op jit(solution)/shard_map/psum | solution.py:117
  18.8 32.7 %collective-permute-start = (f32[1,96,512]{2,1,0:T(8,128)S(1)}, f32[1,96,512]{2,1,0:T(8,128)}, u32[]{:S(2)}, u32[]{:S(2)}) collective-permute-start(f32[1,96,512]{2,1,0:T(8,128)S(1)} %select_bitcast_fusion.29), channel_id=1, source_target_pairs={{0,8},{8,16},{16,24},{24,32},{32,40},{40,48},{48,56},{56,64},{64,7... | collective-permute-start | bytes 589832 | tf_op jit(solution)/shard_map/ppermute | solution.py:22
  23.5 22.6 %collective-permute-start.1 = (f32[1,96,512]{2,1,0:T(8,128)S(1)}, f32[1,96,512]{2,1,0:T(8,128)S(1)}, u32[]{:S(2)}, u32[]{:S(2)}) collective-permute-start(f32[1,96,512]{2,1,0:T(8,128)S(1)} %get-tuple-element.100), channel_id=1, source_target_pairs={{8,0},{16,8},{24,16},{32,24},{40,32},{48,40},{56,48},{64,56},{72,6... | collective-permute-start | bytes 589832 | tf_op jit(solution)/shard_map/ppermute | solution.py:25
  26.8 25.7 %collective-permute-start.2 = (f32[1,96,512]{2,1,0:T(8,128)}, f32[1,96,512]{2,1,0:T(8,128)}, u32[]{:S(2)}, u32[]{:S(2)}) collective-permute-start(f32[1,96,512]{2,1,0:T(8,128)} %select_bitcast_fusion.28), channel_id=1, source_target_pairs={{0,1},{1,2},{2,3},{3,4},{4,5},{5,6},{6,7},{8,9},{9,10},{10,11},{11... | collective-permute-start | bytes 589832 | tf_op jit(solution)/shard_map/ppermute | solution.py:22
  31.1 18.9 collective-permute-start.3
  43.8 17.6 collective-permute-start.21
  46.1 18.3 collective-permute-start.23
  55.5 389.4 %all-reduce.27.cloned.1.call-start = ((), (), s32[]{:S(2)}) async-start(), calls=%async_computation.7 | async-start | bytes 1572864 | tf_op jit(solution)/shard_map/psum | solution.py:117
  208.2 20.4 %collective-permute-start.5 = (f32[1,96,512]{2,1,0:T(8,128)}, f32[1,96,512]{2,1,0:T(8,128)}, u32[]{:S(2)}, u32[]{:S(2)}) collective-permute-start(f32[1,96,512]{2,1,0:T(8,128)} %select_bitcast_fusion.27), channel_id=1, source_target_pairs={{0,8},{8,16},{16,24},{24,32},{32,40},{40,48},{48,56},{56,64},{64,7... | collective-permute-start | bytes 589832 | tf_op jit(solution)/shard_map/ppermute | solution.py:22
  244.7 25.0 %collective-permute-start.20 = (f32[1,96,512]{2,1,0:T(8,128)}, f32[1,96,512]{2,1,0:T(8,128)}, u32[]{:S(2)}, u32[]{:S(2)}) collective-permute-start(f32[1,96,512]{2,1,0:T(8,128)} %get-tuple-element.130), channel_id=1, source_target_pairs={{0,8},{8,16},{16,24},{24,32},{32,40},{40,48},{48,56},{56,64},{64,7... | collective-permute-start | bytes 589832 | tf_op jit(solution)/shard_map/ppermute | solution.py:22
  255.7 18.7 collective-permute-start.22
  260.6 27.6 %collective-permute-start.10 = (f32[1,96,512]{2,1,0:T(8,128)}, f32[1,96,512]{2,1,0:T(8,128)}, u32[]{:S(2)}, u32[]{:S(2)}) collective-permute-start(f32[1,96,512]{2,1,0:T(8,128)} %get-tuple-element.129), channel_id=1, source_target_pairs={{0,8},{8,16},{16,24},{24,32},{32,40},{40,48},{48,56},{56,64},{64,7... | collective-permute-start | bytes 589832 | tf_op jit(solution)/shard_map/ppermute | solution.py:22
  265.0 25.2 %collective-permute-start.12 = (f32[1,96,512]{2,1,0:T(8,128)}, f32[1,96,512]{2,1,0:T(8,128)}, u32[]{:S(2)}, u32[]{:S(2)}) collective-permute-start(f32[1,96,512]{2,1,0:T(8,128)} %get-tuple-element.127), channel_id=1, source_target_pairs={{0,1},{1,2},{2,3},{3,4},{4,5},{5,6},{6,7},{8,9},{9,10},{10,11},{11... | collective-permute-start | bytes 589832 | tf_op jit(solution)/shard_map/ppermute | solution.py:22
  295.8 368.0 %all-reduce.15.cloned.1.call-start = ((), (), s32[]{:S(2)}) async-start(), calls=%async_computation.1 | async-start | bytes 786432 | tf_op jit(solution)/shard_map/psum | solution.py:117
  466.3 37.4 %collective-permute-start.15 = (f32[1,96,512]{2,1,0:T(8,128)}, f32[1,96,512]{2,1,0:T(8,128)}, u32[]{:S(2)}, u32[]{:S(2)}) collective-permute-start(f32[1,96,512]{2,1,0:T(8,128)} %get-tuple-element.123), channel_id=1, source_target_pairs={{0,8},{8,16},{16,24},{24,32},{32,40},{40,48},{48,56},{56,64},{64,7... | collective-permute-start | bytes 589832 | tf_op jit(solution)/shard_map/ppermute | solution.py:22
  470.3 17.5 collective-permute-start.26
  471.6 24.7 %collective-permute-start.18 = (f32[1,96,512]{2,1,0:T(8,128)}, f32[1,96,512]{2,1,0:T(8,128)}, u32[]{:S(2)}, u32[]{:S(2)}) collective-permute-start(f32[1,96,512]{2,1,0:T(8,128)} %get-tuple-element.78), channel_id=1, source_target_pairs={{1,0},{2,1},{3,2},{4,3},{5,4},{6,5},{7,6},{9,8},{10,9},{11,10},{12... | collective-permute-start | bytes 589832 | tf_op jit(solution)/shard_map/ppermute | solution.py:25
  475.9 25.5 %collective-permute-start.28 = (f32[1,96,512]{2,1,0:T(8,128)}, f32[1,96,512]{2,1,0:T(8,128)}, u32[]{:S(2)}, u32[]{:S(2)}) collective-permute-start(f32[1,96,512]{2,1,0:T(8,128)} %get-tuple-element.82), channel_id=1, source_target_pairs={{1,0},{2,1},{3,2},{4,3},{5,4},{6,5},{7,6},{9,8},{10,9},{11,10},{12... | collective-permute-start | bytes 589832 | tf_op jit(solution)/shard_map/ppermute | solution.py:25
  482.8 24.6 %collective-permute-start.27 = (f32[1,96,512]{2,1,0:T(8,128)}, f32[1,96,512]{2,1,0:T(8,128)}, u32[]{:S(2)}, u32[]{:S(2)}) collective-permute-start(f32[1,96,512]{2,1,0:T(8,128)} %get-tuple-element.119), channel_id=1, source_target_pairs={{0,1},{1,2},{2,3},{3,4},{4,5},{5,6},{6,7},{8,9},{9,10},{10,11},{11... | collective-permute-start | bytes 589832 | tf_op jit(solution)/shard_map/ppermute | solution.py:22
  487.8 16.8 collective-permute-start.25
  519.3 386.3 %all-reduce.17.cloned.1.call-start = ((), (), s32[]{:S(2)}) async-start(), calls=%async_computation.2 | async-start | bytes 786432 | tf_op jit(solution)/shard_map/psum | solution.py:117
  672.6 28.5 %collective-permute-start.30 = (f32[1,96,512]{2,1,0:T(8,128)}, f32[1,96,512]{2,1,0:T(8,128)}, u32[]{:S(2)}, u32[]{:S(2)}) collective-permute-start(f32[1,96,512]{2,1,0:T(8,128)} %select_bitcast_fusion.17), channel_id=1, source_target_pairs={{0,8},{8,16},{16,24},{24,32},{32,40},{40,48},{48,56},{56,64},{64,7... | collective-permute-start | bytes 589832 | tf_op jit(solution)/shard_map/ppermute | solution.py:22
  675.2 17.6 collective-permute-start.31
  680.3 17.0 collective-permute-start.33
  685.8 17.2 collective-permute-start.32
  718.3 29.7 %collective-permute-start.35 = (f32[1,96,512]{2,1,0:T(8,128)}, f32[1,96,512]{2,1,0:T(8,128)}, u32[]{:S(2)}, u32[]{:S(2)}) collective-permute-start(f32[1,96,512]{2,1,0:T(8,128)} %select_bitcast_fusion.15), channel_id=1, source_target_pairs={{0,8},{8,16},{16,24},{24,32},{32,40},{40,48},{48,56},{56,64},{64,7... | collective-permute-start | bytes 589832 | tf_op jit(solution)/shard_map/ppermute | solution.py:22
  732.8 17.2 collective-permute-start.37
  757.9 409.2 %all-reduce.19.cloned.1.call-start = ((), (), s32[]{:S(2)}) async-start(), calls=%async_computation.3 | async-start | bytes 786432 | tf_op jit(solution)/shard_map/psum | solution.py:117
  914.3 28.6 %collective-permute-start.40 = (f32[1,96,512]{2,1,0:T(8,128)}, f32[1,96,512]{2,1,0:T(8,128)}, u32[]{:S(2)}, u32[]{:S(2)}) collective-permute-start(f32[1,96,512]{2,1,0:T(8,128)} %select_bitcast_fusion.13), channel_id=1, source_target_pairs={{0,8},{8,16},{16,24},{24,32},{32,40},{40,48},{48,56},{56,64},{64,7... | collective-permute-start | bytes 589832 | tf_op jit(solution)/shard_map/ppermute | solution.py:22
  916.9 17.8 collective-permute-start.41
  922.0 17.2 collective-permute-start.43
  927.5 17.4 collective-permute-start.42
  1025.3 384.6 %all-reduce.21.cloned.1.call-start = ((), (), s32[]{:S(2)}) async-start(), calls=%async_computation.4 | async-start | bytes 786432 | tf_op jit(solution)/shard_map/psum | solution.py:117
  1176.0 28.6 %collective-permute-start.45 = (f32[1,96,512]{2,1,0:T(8,128)}, f32[1,96,512]{2,1,0:T(8,128)}, u32[]{:S(2)}, u32[]{:S(2)}) collective-permute-start(f32[1,96,512]{2,1,0:T(8,128)} %select_bitcast_fusion.11), channel_id=1, source_target_pairs={{0,8},{8,16},{16,24},{24,32},{32,40},{40,48},{48,56},{56,64},{64,7... | collective-permute-start | bytes 589832 | tf_op jit(solution)/shard_map/ppermute | solution.py:22
  1178.6 17.8 collective-permute-start.46
  1183.7 17.2 collective-permute-start.48
  1189.1 17.4 collective-permute-start.47
  1221.9 29.8 %collective-permute-start.50 = (f32[1,96,512]{2,1,0:T(8,128)}, f32[1,96,512]{2,1,0:T(8,128)}, u32[]{:S(2)}, u32[]{:S(2)}) collective-permute-start(f32[1,96,512]{2,1,0:T(8,128)} %select_bitcast_fusion.9), channel_id=1, source_target_pairs={{0,8},{8,16},{16,24},{24,32},{32,40},{40,48},{48,56},{56,64},{64,7... | collective-permute-start | bytes 589832 | tf_op jit(solution)/shard_map/ppermute | solution.py:22
  1236.3 17.3 collective-permute-start.52
  1262.3 409.1 %all-reduce.23.cloned.1.call-start = ((), (), s32[]{:S(2)}) async-start(), calls=%async_computation.5 | async-start | bytes 786432 | tf_op jit(solution)/shard_map/psum | solution.py:117
  1418.6 28.6 %collective-permute-start.55 = (f32[1,96,512]{2,1,0:T(8,128)}, f32[1,96,512]{2,1,0:T(8,128)}, u32[]{:S(2)}, u32[]{:S(2)}) collective-permute-start(f32[1,96,512]{2,1,0:T(8,128)} %select_bitcast_fusion.7), channel_id=1, source_target_pairs={{0,8},{8,16},{16,24},{24,32},{32,40},{40,48},{48,56},{56,64},{64,7... | collective-permute-start | bytes 589832 | tf_op jit(solution)/shard_map/ppermute | solution.py:22
  1421.3 17.8 collective-permute-start.56
  1426.3 17.2 collective-permute-start.58
  1431.8 17.4 collective-permute-start.57
  1529.5 357.1 %all-reduce.25.cloned.1.call-start = ((), (), s32[]{:S(2)}) async-start(), calls=%async_computation.6 | async-start | bytes 786432 | tf_op jit(solution)/shard_map/psum | solution.py:117
  1676.2 19.9 collective-permute-start.60
  1708.0 21.1 %collective-permute-start.65 = (f32[1,96,512]{2,1,0:T(8,128)}, f32[1,96,512]{2,1,0:T(8,128)}, u32[]{:S(2)}, u32[]{:S(2)}) collective-permute-start(f32[1,96,512]{2,1,0:T(8,128)} %select_bitcast_fusion.3), channel_id=1, source_target_pairs={{0,8},{8,16},{16,24},{24,32},{32,40},{40,48},{48,56},{56,64},{64,7... | collective-permute-start | bytes 589832 | tf_op jit(solution)/shard_map/ppermute | solution.py:22
  1895.7 25.9 %collective-permute-start.70 = (f32[1,96,512]{2,1,0:T(8,128)}, f32[1,96,512]{2,1,0:T(8,128)}, u32[]{:S(2)}, u32[]{:S(2)}) collective-permute-start(f32[1,96,512]{2,1,0:T(8,128)} %select_bitcast_fusion.1), channel_id=1, source_target_pairs={{0,8},{8,16},{16,24},{24,32},{32,40},{40,48},{48,56},{56,64},{64,7... | collective-permute-start | bytes 589832 | tf_op jit(solution)/shard_map/ppermute | solution.py:22
  (76 other events, 4004.4 us)
Sparse Core Ops, SparseCore 0:
  55.7 147.7 all-reduce.12
  296.0 148.8 all-reduce.26
  519.4 144.4 all-reduce.14
  758.1 147.3 all-reduce.16
  1025.4 141.7 all-reduce.18
  1262.4 147.4 all-reduce.20
  1529.6 141.7 all-reduce.22
  1739.1 147.4 all-reduce.24
where the time goes:
time: 2020 us; the launch traced here: 2010 us
  waiting for transfers between devices  1160 us (57%)
  local copies, waits for them, and re-layouts  267 us (13%)
  blocking collectives  201 us (10%)
  starting transfers between devices  191 us (9%)
  other arithmetic  106 us (5%)
  matrix products  63.5 us (3%)
    psum x8, waiting for transfers between devices, collect(): lax.psum(placed, ('sub', 'grp')).reshape(domain_count * MODES, load_count)  1150 us
    psum x3, blocking collectives, shards(): lax.psum((inner_sum(gradient, search), inner_sum(search, image_vec), inne...  201 us
    ppermute x30, starting transfers between devices, extended(): lax.ppermute(lax.slice_in_dim(block, block.shape[dim] - width, None, axis...  106 us
    ppermute x30, starting transfers between devices, extended(): lax.ppermute(lax.slice_in_dim(block, 0, width, axis=dim), axis, backward)  66.7 us
  transfers between devices with their start and end apart: 83, of which 18 were waited for; matrix products, arithmetic and copies ran while one was open for 11% of the time, Pallas kernels for 0%

commit v1 on v0

v1 whole, which is shorter than its diff:
```python
import functools

import jax
import jax.numpy as jnp
from jax import lax
from jax.experimental import pallas as pl
from jax.experimental.pallas import tpu as pltpu
from jax.sharding import PartitionSpec as P

FACE = 512
CONT = 256
ORDER = 2560
MODES = 6
NLOAD = 96
ITERS = 3
CON = 4 * FACE
SEGS = ((0, 512), (512, 512), (1024, 512), (1536, 512), (2048, 256), (2304, 256))

F32 = jnp.float32
BF16 = jnp.bfloat16
step_scale = 0.2
AXES = ("sub", "grp")


def sds(shape, dtype=F32):
    return jax.ShapeDtypeStruct(shape, dtype)


def mm(a, b):
    return jnp.dot(a, b, preferred_element_type=F32)


def split2(x):
    hi = x.astype(BF16)
    return hi, (x - hi.astype(F32)).astype(BF16)


def shuffle(x, onehot):
    hi = x.astype(BF16)
    rest = x - hi.astype(F32)
    mid = rest.astype(BF16)
    low = (rest - mid.astype(F32)).astype(BF16)
    return mm(hi, onehot) + mm(mid, onehot) + mm(low, onehot)


def flip(x):
    rows = x.shape[0]
    if rows % 128:
        x = jnp.concatenate([x, jnp.zeros((128 - rows % 128, x.shape[1]), F32)], axis=0)
    return x.T


def cut(width):
    return [(at, min(width, ORDER - at)) for at in range(0, ORDER, width)]


def spread(rows, t_stack):
    hi = rows.astype(BF16).astype(F32)
    stack = jnp.concatenate([hi, hi, rows - hi, jnp.zeros((112, 128), F32)], axis=0)
    return stack.T[:NLOAD].astype(BF16)


def coarse(vh, vl, g):
    gh, gl = split2(g)
    return mm(vh, gh) + mm(vl, gh) + mm(vh, gl)


def project_rows(x, bh, bl):
    xh, xl = split2(x)
    return mm(xh, bh) + mm(xl, bh) + mm(xh, bl)


def lanesum(x):
    return jnp.sum(x, axis=1, keepdims=True)


def message(coef_t, first, second):
    lane = lax.broadcasted_iota(jnp.int32, coef_t.shape, 1)
    full = jnp.where(lane == 6, first, jnp.where(lane == 7, second, coef_t))
    return flip(full)[:8]


def prepare_kernel(
    basis, vp, coeff, srow, scol, grow, gcol, crow, ccol, flags,
    a_s, at_s, a_g, at_g, a_c, at_c, basis_out, act_out, m0, m1, m2, m3, mc,
):
    for row, col, a, at in ((srow, scol, a_s, at_s), (grow, gcol, a_g, at_g), (crow, ccol, a_c, at_c)):
        n = row.shape[1]
        a[...] = (lax.broadcasted_iota(jnp.int32, (n, n), 1) == col[...]).astype(F32).astype(BF16)
        at[...] = (lax.broadcasted_iota(jnp.int32, (n, n), 0) == row[...]).astype(F32).astype(BF16)
    parts = [
        basis[:, 0:512],
        shuffle(basis[:, 512:1024], a_s[...]),
        basis[:, 1024:1536],
        shuffle(basis[:, 1536:2048], a_g[...]),
        shuffle(basis[:, 2048:2304], a_c[...]),
        basis[:, 2304:2560],
    ]
    for (at, width), part in zip(SEGS, parts):
        basis_out[:, at : at + width] = part
    act_out[...] = mm(flags[...].astype(F32).astype(BF16), a_c[...])
    for ref, part in zip((m0, m1, m2, m3), parts):
        ref[0:8, :] = part
        ref[8:16, :] = vp[:, 0:512]
        ref[16:24, :] = vp[:, 512:1024]
        ref[24:32, :] = jnp.zeros((8, 512), F32)
        ref[24:32, 0:128] = coeff[...]
    mc[0:8, :] = parts[4]
    for k in range(4):
        mc[8 + 8 * k : 16 + 8 * k, :] = vp[:, 256 * k : 256 * k + 256]
    mc[40:48, :] = jnp.zeros((8, 256), F32)
    mc[40:48, 0:128] = coeff[...]


def start_kernel(
    basis, vp, coeff, r0, r1, r2, r3, rc,
    t_stack, vh, vl, bh, bl, point, msg,
):
    zero8 = jnp.zeros((8, ORDER), F32)
    pieces = [basis[...]]
    for ref, at in ((r0, 0), (r1, 512), (r2, 1024), (r3, 1536)):
        left = [zero8[:, :at]] if at else []
        pieces.append(jnp.concatenate(left + [ref[0:8, :], zero8[:, at + 512 :]], axis=1))
    pieces.append(jnp.concatenate([zero8[:, :CON], rc[0:8, :], zero8[:, CON + CONT :]], axis=1))
    t = jnp.concatenate(pieces, axis=0)
    th, tl = split2(t)
    t_stack[0:48, :] = th
    t_stack[48:96, :] = tl
    t_stack[96:144, :] = th
    t_stack[144:256, :] = jnp.zeros((112, ORDER), BF16)
    rows = [vp[...]]
    coefs = [coeff[...]]
    for ref in (r0, r1, r2, r3):
        rows.append(jnp.concatenate([ref[8:16, :], ref[16:24, :]], axis=1))
        coefs.append(ref[24:32, 0:128])
    rows.append(jnp.concatenate([rc[8 + 8 * k : 16 + 8 * k, :] for k in range(4)], axis=1))
    coefs.append(rc[40:48, 0:128])
    hi, low = split2(jnp.concatenate(rows, axis=0))
    vh[...] = hi
    vl[...] = low
    bhi, blow = split2(flip(basis[...]))
    bh[...] = bhi
    bl[...] = blow
    factor = spread(jnp.concatenate(coefs, axis=0), t_stack)
    coef_t = jnp.zeros((NLOAD, 128), F32)
    for at, width in SEGS:
        seg = slice(at, at + width)
        x = mm(factor, t_stack[:, seg])
        if at == CON:
            x = jnp.maximum(x, 0.0)
        point[:, seg] = x
        coef_t += project_rows(x, bh[seg, :], bl[seg, :])
    msg[...] = flip(coef_t)[:8]


def rounded_rows(p, seg, at_s, at_g, at_c):
    p = p.astype(BF16)
    back = {512: at_s, 1536: at_g, 2048: at_c}.get(seg)
    if back is not None:
        p = mm(p, back[...]).astype(BF16)
    return p


def first_search_kernel(
    g, vh, vl, u, t_stack, a_s, at_s, at_g, at_c, schur,
    gh, gl, p, z0, z1,
):
    step = pl.program_id(0)

    @pl.when(step == 0)
    def _():
        column = flip(g[...])[96:112]
        row = lax.broadcasted_iota(jnp.int32, column.shape, 0)
        hi, low = split2(jnp.where(row < MODES, column, 0.0))
        gh[...] = hi
        gl[...] = low
        factor = spread(coarse(vh[...], vl[...], g[...]), t_stack)
        for at, width in SEGS:
            seg = slice(at, at + width)
            p[:, seg] = rounded_rows(u[:, seg] - mm(factor, t_stack[:, seg]), at, at_s, at_g, at_c)
        z0[...] = mm(p[...], schur[...])

    @pl.when(step == 1)
    def _():
        z1[...] = shuffle(mm(p[...], schur[...]), a_s[...])


def search_kernel(
    k, g, vh, vl, gh, gl, codes, scal, prev, u, d, t_stack, a_s, at_s, at_g, at_c, schur,
    q, p, coef_u, coef_q, scal_out, z0, z1,
):
    step = pl.program_id(0)

    @pl.when(step == 0)
    def _():
        got = g[...]
        gah, gal = split2(got)
        alpha = mm(vh[...], gah) + mm(vl[...], gah) + mm(vh[...], gal)
        gamma = (mm(gh[...], gah) + mm(gl[...], gah) + mm(gh[...], gal))[:8]
        sums = jnp.sum(got.reshape(128, 8, 128), axis=0)
        coef = jnp.concatenate([alpha, gamma], axis=0)
        coef_u[...] = coef
        scal_out[0:1, :] = sums[7:8]
        scal_out[1:8, :] = jnp.zeros((7, 128), F32)
        if k > 0:
            bend = sums[6:7]
            length, curve, cross = scal[0:1], scal[1:2], scal[2:3]
            both = (codes[k : k + 1] == 0) & (codes[k - 1 : k] == 0)
            factor2 = jnp.where(both, (cross - length * bend) / curve, 0.0)
            mix = jnp.where(factor2 == 0.0, coef, coef - factor2 * prev[...])
            coef_q[...] = mix
            g2 = flip(jnp.broadcast_to(factor2, (8, 128)))[:NLOAD, 0:1]
        else:
            mix = coef
            coef_q[...] = coef
        factor = spread(mix[:48], t_stack)
        for at, width in SEGS:
            seg = slice(at, at + width)
            x = u[:, seg]
            if k > 0:
                x = x - g2 * d[:, seg]
            q[:, seg] = x
            p[:, seg] = rounded_rows(x - mm(factor, t_stack[:, seg]), at, at_s, at_g, at_c)
        z0[...] = mm(p[...], schur[...])

    @pl.when(step == 1)
    def _():
        z1[...] = shuffle(mm(p[...], schur[...]), a_s[...])


def product_kernel(p, a_g, a_c, schur, z2, z3, zc, zd):
    step = pl.program_id(0)
    z = mm(p[...], schur[...])

    @pl.when(step == 0)
    def _():
        z2[...] = z

    @pl.when(step == 1)
    def _():
        z3[...] = shuffle(z, a_g[...])

    @pl.when(step == 2)
    def _():
        zc[...] = shuffle(z[:, :CONT], a_c[...])
        zd[...] = z[:, CONT:]


def image_kernel(
    z0, z1, z2, z3, zc, zd, r0, r1, r2, r3, rc, q, u, weight, coef_u, coef_q, bh, bl,
    image, msg,
):
    coef_t = jnp.zeros((NLOAD, 128), F32)
    curve = jnp.zeros((NLOAD, 1), F32)
    cross = jnp.zeros((NLOAD, 1), F32)
    pairs = ((z0, r0), (z1, r1), (z2, r2), (z3, r3), (zc, rc), (zd, None))
    for (at, width), (own, got) in zip(SEGS, pairs):
        seg = slice(at, at + width)
        x = own[...] if got is None else own[...] + got[...]
        image[:, seg] = x
        coef_t += project_rows(x, bh[seg, :], bl[seg, :])
        xw = x * weight[:, seg]
        curve += lanesum(q[:, seg] * xw)
        cross += lanesum(u[:, seg] * xw)
    rows = message(coef_t, curve, cross)
    row = lax.broadcasted_iota(jnp.int32, (8, 128), 0)
    modes = jnp.where(row < MODES, rows, 0.0)
    fix_q = jnp.sum(coef_q[48:56] * modes, axis=0, keepdims=True)
    fix_u = jnp.sum(coef_u[48:56] * modes, axis=0, keepdims=True)
    msg[...] = rows - jnp.where(row == 6, fix_q, 0.0) - jnp.where(row == 7, fix_u, 0.0)


def less_load_kernel(z0, z1, z2, z3, zc, zd, load, a_s, a_g, a_c, o0, o1, o2, o3, oc, od):
    pairs = ((z0, o0, None), (z1, o1, a_s), (z2, o2, None), (z3, o3, a_g), (zc, oc, a_c), (zd, od, None))
    for (at, width), (own, out, order) in zip(SEGS, pairs):
        x = load[:, at : at + width]
        out[...] = own[...] - (x if order is None else shuffle(x, order[...]))


def first_image_kernel(
    z0, z1, z2, z3, zc, zd, r0, r1, r2, r3, rc, bh, bl,
    image, msg,
):
    coef_t = jnp.zeros((NLOAD, 128), F32)
    pairs = ((z0, r0), (z1, r1), (z2, r2), (z3, r3), (zc, rc), (zd, None))
    for (at, width), (own, got) in zip(SEGS, pairs):
        seg = slice(at, at + width)
        x = own[...] if got is None else own[...] + got[...]
        image[:, seg] = x
        coef_t += project_rows(x, bh[seg, :], bl[seg, :])
    msg[...] = flip(coef_t)[:8]


def next_part(seg, at, codes, m, g, w, act, weight):
    bent = w * w
    if at == CON:
        free = 1.0 - act
        free_grad = free * g
        bent = free * bent
        chopped = act * jnp.minimum(g, 0.0)
        trial = jnp.maximum(m - step_scale * free_grad, 0.0)
    else:
        free_grad = g
        chopped = 0.0
        trial = m - step_scale * g
    u = jnp.where(codes == 0, free_grad, jnp.where(codes == 2, chopped, trial - m))
    return u, lanesum(g * u * weight), lanesum(bent * weight)


def first_update_kernel(
    g, vh, vl, codes, point, image, act, weight, t_stack, bh, bl,
    gradient, u, msg,
):
    factor = spread(coarse(vh[...], vl[...], g[...]), t_stack)
    code = codes[:, 0:1]
    coef_t = jnp.zeros((NLOAD, 128), F32)
    slope = jnp.zeros((NLOAD, 1), F32)
    for at, width in SEGS:
        seg = slice(at, at + width)
        grad = image[:, seg] - mm(factor, t_stack[:, seg])
        gradient[:, seg] = grad
        x, slope_part, _ = next_part(seg, at, code, point[:, seg], grad, grad, act[...], weight[:, seg])
        u[:, seg] = x
        slope += slope_part
        coef_t += project_rows(x, bh[seg, :], bl[seg, :])
    msg[...] = message(coef_t, jnp.zeros((NLOAD, 1), F32), slope)


def lengths(k, g, codes_rows, scal):
    sums = jnp.sum(g.reshape(128, 8, 128), axis=0)
    curve, cross = sums[6:7], sums[7:8]
    length = jnp.where(codes_rows[k : k + 1] == 1, -1.0, scal[0:1] / curve)
    return length, curve, cross


def update_kernel(
    k, g, vh, vl, codes, codes_rows, scal, point, gradient, q, image, act, weight, t_stack, bh, bl,
    point_out, gradient_out, u, scal_out, msg,
):
    got = g[...]
    length, curve, cross = lengths(k, got, codes_rows, scal)
    scal_out[0:1, :] = length
    scal_out[1:2, :] = curve
    scal_out[2:3, :] = cross
    scal_out[3:8, :] = jnp.zeros((5, 128), F32)
    step = flip(jnp.broadcast_to(length, (8, 128)))[:NLOAD, 0:1]
    factor = spread(coarse(vh[...], vl[...], got), t_stack)
    code = codes[:, k + 1 : k + 2]
    coef_t = jnp.zeros((NLOAD, 128), F32)
    slope = jnp.zeros((NLOAD, 1), F32)
    bend = jnp.zeros((NLOAD, 1), F32)
    for at, width in SEGS:
        seg = slice(at, at + width)
        w = image[:, seg] - mm(factor, t_stack[:, seg])
        m = point[:, seg] - step * q[:, seg]
        grad = gradient[:, seg] - step * w
        point_out[:, seg] = m
        gradient_out[:, seg] = grad
        x, slope_part, bend_part = next_part(seg, at, code, m, grad, w, act[...], weight[:, seg])
        u[:, seg] = x
        slope += slope_part
        bend += bend_part
        coef_t += project_rows(x, bh[seg, :], bl[seg, :])
    msg[...] = message(coef_t, bend, slope)


def last_update_kernel(
    k, g, vh, vl, codes_rows, scal, point, gradient, q, image, t_stack, at_s, at_g, at_c,
    point_out, gradient_out,
):
    got = g[...]
    length, _, _ = lengths(k, got, codes_rows, scal)
    step = flip(jnp.broadcast_to(length, (8, 128)))[:NLOAD, 0:1]
    factor = spread(coarse(vh[...], vl[...], got), t_stack)
    for at, width in SEGS:
        seg = slice(at, at + width)
        w = image[:, seg] - mm(factor, t_stack[:, seg])
        m = point[:, seg] - step * q[:, seg]
        grad = gradient[:, seg] - step * w
        back = {512: at_s, 1536: at_g, 2048: at_c}.get(at)
        if back is not None:
            m = shuffle(m, back[...])
            grad = shuffle(grad, back[...])
        point_out[:, seg] = m
        gradient_out[:, seg] = grad


def call(kernel, outs, *operands, flops=0):
    moved = sum(x.size * x.dtype.itemsize for x in operands) + sum(
        o.size * o.dtype.itemsize for o in outs
    )
    return pl.pallas_call(
        kernel,
        out_shape=outs,
        compiler_params=pltpu.CompilerParams(vmem_limit_bytes=48 * 2**20),
        cost_estimate=pl.CostEstimate(flops=flops, bytes_accessed=moved, transcendentals=0),
    )(*operands)


def whole(shape):
    return pl.BlockSpec(shape, lambda i: (0,) * len(shape))


def call_columns(kernel, outs, first, count, *operands):
    schur = operands[-1]
    moved = sum(x.size * x.dtype.itemsize for x in operands[:-1]) + count * FACE * ORDER * 2
    return pl.pallas_call(
        kernel,
        grid=(count,),
        in_specs=[whole(x.shape) for x in operands[:-1]]
        + [pl.BlockSpec((ORDER, FACE), lambda i: (0, first + i))],
        out_specs=[whole(o.shape) for o in outs],
        out_shape=outs,
        compiler_params=pltpu.CompilerParams(vmem_limit_bytes=48 * 2**20),
        cost_estimate=pl.CostEstimate(
            flops=2 * NLOAD * ORDER * FACE * count, bytes_accessed=moved, transcendentals=0
        ),
    )(*operands)


def shards(
    schur,
    coarse_basis,
    coarse_inverse,
    coarse_coeff,
    dual_load,
    face_order,
    contact_partner,
    active_flags,
    step_codes,
):
    subs, groups = lax.axis_size("sub"), lax.axis_size("grp")
    count = subs * groups
    quarter = groups // 4
    i, j = lax.axis_index("sub"), lax.axis_index("grp")
    sub_up = [(s, s + 1) for s in range(subs - 1)]
    grp_up = [(s, s + 1) for s in range(groups - 1) if s + 1 not in (quarter, 3 * quarter)]
    sub_down = [(b, a) for a, b in sub_up]
    grp_down = [(b, a) for a, b in grp_up]
    across = [(s, (s + groups // 2) % groups) for s in range(groups)]

    def exchange(s0, s1, s2, s3, sc):
        r0 = lax.ppermute(s1, "sub", sub_up)
        r1 = lax.ppermute(s0, "sub", sub_down)
        r2 = lax.ppermute(s3, "grp", grp_up)
        r3 = lax.ppermute(s2, "grp", grp_down)
        rc = lax.ppermute(sc, "grp", across)
        return r0, r1, r2, r3, rc

    def gathered(rows):
        return lax.all_to_all(rows, AXES, 0, 0).reshape(count * 8, 128)

    def everywhere(msg):
        return gathered(jnp.broadcast_to(msg[None], (count, 8, 128)))

    def half(flag):
        return jnp.where(flag, 0.5, 1.0).astype(F32)

    def tall(x):
        return jnp.full((1, x[1]), x[0], F32)

    schur_block = schur[0]
    lower_g = (j > 0) & (j != quarter) & (j != 3 * quarter)
    upper_g = (j < groups - 1) & (j != quarter - 1) & (j != 3 * quarter - 1)
    weight = jnp.concatenate(
        [
            tall((half(i > 0), FACE)),
            tall((half(i < subs - 1), FACE)),
            tall((half(lower_g), FACE)),
            tall((half(upper_g), FACE)),
            tall((0.5, CONT)),
            tall((1.0, ORDER - CON - CONT)),
        ],
        axis=1,
    )
    basis = jnp.pad(coarse_basis[0], ((0, 2), (0, 0)))
    coeff = jnp.pad(coarse_coeff[0], ((0, 2), (0, 128 - NLOAD)))
    blocks = coarse_inverse.reshape(MODES, count, MODES)
    vp = jnp.pad(blocks, ((0, 2), (0, 0), (0, 2))).reshape(8, count * 8)
    columns = jnp.pad(blocks.transpose(1, 0, 2), ((0, 0), (0, 2), (NLOAD, 128 - NLOAD - MODES)))
    codes_rows = jnp.pad(step_codes.T, ((0, 8 - ITERS), (0, 128 - NLOAD)))
    partner = jnp.where(j >= groups // 2, contact_partner[0], jnp.arange(CONT, dtype=jnp.int32))

    orders = []
    for order in (face_order[0, 0], face_order[0, 1], partner):
        orders += [order[None, :], order[:, None]]
    sq = [sds((n, n), BF16) for n in (FACE, FACE, FACE, FACE, CONT, CONT)]
    a_s, at_s, a_g, at_g, a_c, at_c, basis, act, m0, m1, m2, m3, mc = call(
        prepare_kernel,
        sq + [sds((8, ORDER)), sds((NLOAD, CONT))] + [sds((32, FACE))] * 4 + [sds((48, CONT))],
        basis, vp, coeff, *orders, active_flags[0],
    )
    t_stack, vh, vl, bh, bl, point, msg = call(
        start_kernel,
        [
            sds((256, ORDER), BF16),
            sds((48, count * 8), BF16),
            sds((48, count * 8), BF16),
            sds((ORDER, 128), BF16),
            sds((ORDER, 128), BF16),
            sds((NLOAD, ORDER)),
            sds((8, 128)),
        ],
        basis, vp, coeff, *exchange(m0, m1, m2, m3, mc),
    )
    field = sds((NLOAD, ORDER))
    faces = [sds((NLOAD, FACE))] * 2
    rest = [sds((NLOAD, FACE))] * 2 + [sds((NLOAD, CONT))] * 2
    rounded = sds((NLOAD, ORDER), BF16)

    got = gathered(msg[None] + columns)
    gh, gl, p, z0, z1 = call_columns(
        first_search_kernel,
        [sds((16, count * 8), BF16)] * 2 + [rounded] + faces,
        0, 2,
        got, vh, vl, point, t_stack, a_s, at_s, at_g, at_c, schur_block,
    )
    z2, z3, zc, zd = call_columns(product_kernel, rest, 2, 3, p, a_g, a_c, schur_block)
    z0, z1, z2, z3, zc, zd = call(
        less_load_kernel,
        faces + rest,
        z0, z1, z2, z3, zc, zd, dual_load[0], a_s, a_g, a_c,
    )
    image, msg = call(
        first_image_kernel,
        [field, sds((8, 128))],
        z0, z1, z2, z3, zc, zd, *exchange(z0, z1, z2, z3, zc), bh, bl,
    )
    got = everywhere(msg)
    gradient, u, msg = call(
        first_update_kernel,
        [field, field, sds((8, 128))],
        got, vh, vl, step_codes, point, image, act, weight, t_stack, bh, bl,
    )
    q = u
    scal = jnp.zeros((8, 128), F32)
    coef_q = jnp.zeros((56, 128), F32)
    for k in range(ITERS):
        got = everywhere(msg)
        q, p, coef_u, coef_q, scal, z0, z1 = call_columns(
            functools.partial(search_kernel, k),
            [field, rounded, sds((56, 128)), sds((56, 128)), sds((8, 128))] + faces,
            0, 2,
            got, vh, vl, gh, gl, codes_rows, scal, coef_q, u, q, t_stack, a_s, at_s, at_g, at_c,
            schur_block,
        )
        z2, z3, zc, zd = call_columns(product_kernel, rest, 2, 3, p, a_g, a_c, schur_block)
        image, msg = call(
            image_kernel,
            [field, sds((8, 128))],
            z0, z1, z2, z3, zc, zd, *exchange(z0, z1, z2, z3, zc),
            q, u, weight, coef_u, coef_q, bh, bl,
        )
        got = everywhere(msg)
        if k < ITERS - 1:
            point, gradient, u, scal, msg = call(
                functools.partial(update_kernel, k),
                [field, field, field, sds((8, 128)), sds((8, 128))],
                got, vh, vl, step_codes, codes_rows, scal, point, gradient, q, image, act, weight,
                t_stack, bh, bl,
            )
        else:
            point, gradient = call(
                functools.partial(last_update_kernel, k),
                [field, field],
                got, vh, vl, codes_rows, scal, point, gradient, q, image, t_stack, at_s, at_g, at_c,
            )
    return (point[None], gradient[None])


def solution(mesh):
    in_specs = (
        P(AXES, None, None),
        P(AXES, None, None),
        P(AXES, None),
        P(AXES, None, None),
        P(AXES, None, None),
        P(AXES, None, None),
        P(AXES, None),
        P(AXES, None, None),
        P(),
    )
    out_specs = (P(AXES, None, None), P(AXES, None, None))
    return jax.shard_map(shards, mesh=mesh, in_specs=in_specs, out_specs=out_specs, check_vma=False)
```

time: 2020 us -> 332 us (0.16)
  waiting for transfers between devices: 1160 us -> 48.3 us
  local copies, waits for them, and re-layouts: 267 us -> 22.5 us
  starting transfers between devices: 191 us -> 67.3 us
  other arithmetic: 106 us -> 0.2 us
  blocking collectives: 201 us -> 126 us
  Pallas kernels: 0 us -> 64.6 us
  matrix products: 63.5 us -> 0 us
    psum x8 -> x0, waiting for transfers between devices: 1150 us -> none  [collect(): lax.psum(placed, ('sub', 'grp')).reshape(domain_count * MODES, load_count)]
    psum x3 -> x0, blocking collectives: 201 us -> none  [shards(): lax.psum((inner_sum(gradient, search), inner_sum(search, image_vec), inne...]
    gather x150 -> x0, local copies, waits for them, and re-layouts: 149 us -> none  [the longest x30 36 us: received(): from_upper = jnp.take(padded[3], sub_order, axis=1)]
    ppermute x75 -> x25, starting transfers between devices: 191 us -> 55.7 us  [the longest x5 20.6 us: exchange(): r0 = lax.ppermute(s1, 'sub', sub_up)]
    all_to_all x0 -> x6, blocking collectives: none -> 126 us  [gathered(): return lax.all_to_all(rows, AXES, 0, 0).reshape(count * 8, 128)]
    pallas_call x0 -> x19, Pallas kernels: none -> 64.6 us  [the longest x8 38.9 us: call_columns(): pl.pallas_call(kernel, grid=(count,), in_specs=[whole(x.shape) for x in o...]
    dot_general x32 -> x0, matrix products: 63.5 us -> none  [the longest x4 28.7 us: operator(): product = jnp.dot(rounded, schur_block, preferred_element_type=jnp.float32)]
    unnamed x59 -> x0, other arithmetic: 36 us -> none
  transfers between devices with their start and end apart: 83 -> 27, of which waited for: 18 -> 7; matrix products, arithmetic and copies ran while one was open for 11% -> 0% of each run, Pallas kernels for 0% -> 0%
where the time goes in v1:
time: 332 us; the launch traced here: 330 us
  blocking collectives  126 us (38%)
  starting transfers between devices  67.3 us (20%)
  Pallas kernels  64.6 us (19%)
  waiting for transfers between devices  48.3 us (15%)
  local copies, waits for them, and re-layouts  22.5 us (7%)
    all_to_all x6, blocking collectives, gathered(): return lax.all_to_all(rows, AXES, 0, 0).reshape(count * 8, 128)  126 us
    pallas_call x8, Pallas kernels, call_columns(): pl.pallas_call(kernel, grid=(count,), in_specs=[whole(x.shape) for x in o...  38.9 us
    all_to_all x2, waiting for transfers between devices, gathered(): return lax.all_to_all(rows, AXES, 0, 0).reshape(count * 8, 128)  27.2 us
    pallas_call x11, Pallas kernels, call(): pl.pallas_call(kernel, out_shape=outs, compiler_params=pltpu.CompilerPara...  25.7 us
    ppermute x5, waiting for transfers between devices, exchange(): rc = lax.ppermute(sc, 'grp', across)  21.1 us
    ppermute x5, starting transfers between devices, exchange(): r0 = lax.ppermute(s1, 'sub', sub_up)  20.6 us
    unnamed x74, local copies, waits for them, and re-layouts  17 us
    ppermute x5, starting transfers between devices, exchange(): r3 = lax.ppermute(s2, 'grp', grp_down)  16.8 us
  transfers between devices with their start and end apart: 27, of which 7 were waited for; matrix products, arithmetic and copies ran while one was open for 0% of the time, Pallas kernels for 0%

profile of v1, /device:TPU:1, one launch (start us, length us, event | category | flops | bytes accessed | tf_op | source)
XLA Modules:
  0.0 330.0 jit_solution(11692716497456131707)
XLA Ops:
  8.3 3.9 %collective-permute-start = (f32[32,512]{1,0:T(8,128)S(1)}, f32[32,512]{1,0:T(8,128)S(1)}, u32[]{:S(2)}, u32[]{:S(2)}) collective-permute-start(f32[32,512]{1,0:T(8,128)S(1)} %get-tuple-element.94), channel_id=1, source_target_pairs={{0,8},{8,16},{16,24},{24,32},{32,40},{40,48},{48,56},{56,64},{64,7... | collective-permute-start | bytes 196616 | tf_op jit(solution)/shard_map/ppermute | solution.py:443
  12.3 1.3 collective-permute-start.1
  13.6 1.3 collective-permute-start.2
  14.9 3.0 collective-permute-start.3
  17.9 4.8 %collective-permute-start.4 = (f32[48,256]{1,0:T(8,128)S(1)}, f32[48,256]{1,0:T(8,128)S(1)}, u32[]{:S(2)}, u32[]{:S(2)}) collective-permute-start(f32[48,256]{1,0:T(8,128)S(1)} %get-tuple-element.98), channel_id=1, source_target_pairs={{0,4},{1,5},{2,6},{3,7},{4,0},{5,1},{6,2},{7,3},{8,12},{9,13},{10,... | collective-permute-start | bytes 147464 | tf_op jit(solution)/shard_map/ppermute | solution.py:447
  22.7 1.5 collective-permute-done.4.rc
  24.3 1.7 shard_map.105
  26.5 26.6 %all_to_all.40 = f32[128,8,128]{2,1,0:T(8,128)S(1)} all-to-all(f32[128,8,128]{2,1,0:T(8,128)S(1)} %copy.25), channel_id=1, replica_groups=mesh['sub'=16,'grp'=8] {'sub','grp'}, dimensions={0} | all-to-all | bytes 1048576 | tf_op jit(solution)/shard_map/all_to_all | solution.py:451
  53.1 4.2 %shard_map.106 = (bf16[16,1024]{1,0:T(8,128)(2,1)S(1)}, bf16[16,1024]{1,0:T(8,128)(2,1)S(1)}, bf16[96,2560]{1,0:T(8,128)(2,1)S(1)}, f32[96,512]{1,0:T(8,128)S(1)}, f32[96,512]{1,0:T(8,128)S(1)}) custom-call(f32[1024,128]{1,0:T(8,128)S(1)} %bitcast.33, bf16[48,1024]{1,0:T(8,128)(2,1)S(1)} %get-tuple-element.100.vh, ...), custom_call_target="tpu_custom_call" | custom-call | flops 503316480 | bytes 9961472 | tf_op jit(solution)/shard_map/pallas_call | solution.py:407
  57.4 4.9 %shard_map.107 = (f32[96,512]{1,0:T(8,128)S(1)}, f32[96,512]{1,0:T(8,128)S(1)}, f32[96,256]{1,0:T(8,128)S(1)}, f32[96,256]{1,0:T(8,128)S(1)}) custom-call(bf16[96,2560]{1,0:T(8,128)(2,1)S(1)} %get-tuple-element.110.p, bf16[512,512]{1,0:T(8,128)(2,1)S(1)} %get-tuple-element.111.a_g, bf16[256,256]{1,0:T(8,128)(2,1)S(1)} %get-tuple-element.112.a_c, ...), custom_call_target="tpu_custom_call" | custom-call | flops 754974720 | bytes 9011200 | tf_op jit(solution)/shard_map/pallas_call | solution.py:407
  62.3 1.4 shard_map.108
  65.7 4.7 %collective-permute-start.5 = (f32[96,512]{1,0:T(8,128)S(1)}, f32[96,512]{1,0:T(8,128)}, u32[]{:S(2)}, u32[]{:S(2)}) collective-permute-start(f32[96,512]{1,0:T(8,128)S(1)} %get-tuple-element.118.z1), channel_id=1, source_target_pairs={{0,8},{8,16},{16,24},{24,32},{32,40},{40,48},{48,56},{56,64},{64,7... | collective-permute-start | bytes 589832 | tf_op jit(solution)/shard_map/ppermute | solution.py:443
  70.4 4.4 %collective-permute-start.8 = (f32[96,512]{1,0:T(8,128)S(1)}, f32[96,512]{1,0:T(8,128)}, u32[]{:S(2)}, u32[]{:S(2)}) collective-permute-start(f32[96,512]{1,0:T(8,128)S(1)} %get-tuple-element.119.z2), channel_id=1, source_target_pairs={{1,0},{3,2},{4,3},{5,4},{7,6},{9,8},{11,10},{12,11},{13,12},{15,14... | collective-permute-start | bytes 589832 | tf_op jit(solution)/shard_map/ppermute | solution.py:446
  76.3 4.9 %collective-permute-done.9.rc = f32[96,256]{1,0:T(8,128)S(1)} collective-permute-done((f32[96,256]{1,0:T(8,128)S(1)}, f32[96,256]{1,0:T(8,128)S(1)}, u32[]{:S(2)}, u32[]{:S(2)}) %collective-permute-start.9) | collective-permute-done | bytes 98336 | tf_op jit(solution)/shard_map/ppermute | solution.py:447
  82.1 1.9 shard_map.109
  85.8 6.8 %all-to-all-start.1 = ((f32[128,8,128]{2,1,0:T(8,128)}), f32[128,8,128]{2,1,0:T(8,128)S(1)}, u32[]{:S(2)}, u32[]{:S(2)}) async-start(f32[128,8,128]{2,1,0:T(8,128)} %broadcast_in_dim.34), calls=%async_computation.1 | async-start | bytes 1048576 | tf_op jit(solution)/shard_map/all_to_all | solution.py:451
  92.7 13.5 %all-to-all-done.1 = f32[128,8,128]{2,1,0:T(8,128)S(1)} async-done(((f32[128,8,128]{2,1,0:T(8,128)}), f32[128,8,128]{2,1,0:T(8,128)S(1)}, u32[]{:S(2)}, u32[]{:S(2)}) %all-to-all-start.1) | async-done | bytes 524320 | tf_op jit(solution)/shard_map/all_to_all | solution.py:451
  109.5 3.3 %shard_map.110 = (f32[96,2560]{1,0:T(8,128)S(1)}, f32[96,2560]{1,0:T(8,128)S(1)}, f32[8,128]{1,0:T(8,128)S(1)}) custom-call(f32[1024,128]{1,0:T(8,128)S(1)} %bitcast.30, bf16[48,1024]{1,0:T(8,128)(2,1)S(1)} %get-tuple-element.100.vh, bf16[48,1024]{1,0:T(8,128)(2,1)S(1)} %get-tuple-element.101.vl, s32[96,3]{1,0:T(8,128)S(1)} %copy.26.codes, ...), custom_call_target="tpu_custom_call" | custom-call | bytes 7388288 | tf_op jit(solution)/shard_map/pallas_call | solution.py:392
  115.6 4.8 %all-to-all-start.2 = ((f32[128,8,128]{2,1,0:T(8,128)}), f32[128,8,128]{2,1,0:T(8,128)S(1)}, u32[]{:S(2)}, u32[]{:S(2)}) async-start(f32[128,8,128]{2,1,0:T(8,128)} %broadcast_in_dim.82), calls=%async_computation.2 | async-start | bytes 1048576 | tf_op jit(solution)/shard_map/all_to_all | solution.py:451
  120.4 13.7 %all-to-all-done.2 = f32[128,8,128]{2,1,0:T(8,128)S(1)} async-done(((f32[128,8,128]{2,1,0:T(8,128)}), f32[128,8,128]{2,1,0:T(8,128)S(1)}, u32[]{:S(2)}, u32[]{:S(2)}) %all-to-all-start.2) | async-done | bytes 524320 | tf_op jit(solution)/shard_map/all_to_all | solution.py:451
  140.2 4.5 %shard_map.111 = (f32[96,2560]{1,0:T(8,128)S(1)}, bf16[96,2560]{1,0:T(8,128)(2,1)S(1)}, f32[56,128]{1,0:T(8,128)S(1)}, f32[56,128]{1,0:T(8,128)S(1)}, f32[8,128]...) custom-call(f32[1024,128]{1,0:T(8,128)S(1)} %bitcast.35, bf16[48,1024]{1,0:T(8,128)(2,1)S(1)} %get-tuple-element.100.vh, ...), custom_call_target="tpu_custom_call" | custom-call | flops 503316480 | bytes 11046912 | tf_op jit(solution)/shard_map/pallas_call | solution.py:407
  144.7 5.3 %shard_map.112 = (f32[96,512]{1,0:T(8,128)S(1)}, f32[96,512]{1,0:T(8,128)S(1)}, f32[96,256]{1,0:T(8,128)S(1)}, f32[96,256]{1,0:T(8,128)S(1)}) custom-call(bf16[96,2560]{1,0:T(8,128)(2,1)S(1)} %get-tuple-element.134.p, bf16[512,512]{1,0:T(8,128)(2,1)S(1)} %get-tuple-element.111.a_g, bf16[256,256]{1,0:T(8,128)(2,1)S(1)} %get-tuple-element.112.a_c, ...), custom_call_target="tpu_custom_call" | custom-call | flops 754974720 | bytes 9011200 | tf_op jit(solution)/shard_map/pallas_call | solution.py:407
  150.0 3.1 collective-permute-start.13
  153.2 1.3 collective-permute-start.12
  154.5 1.3 collective-permute-start.11
  155.8 4.0 %collective-permute-start.10 = (f32[96,512]{1,0:T(8,128)S(1)}, f32[96,512]{1,0:T(8,128)S(1)}, u32[]{:S(2)}, u32[]{:S(2)}) collective-permute-start(f32[96,512]{1,0:T(8,128)S(1)} %get-tuple-element.133.z1), channel_id=1, source_target_pairs={{0,8},{8,16},{16,24},{24,32},{32,40},{40,48},{48,56},{56,64},{64,7... | collective-permute-start | bytes 589832 | tf_op jit(solution)/shard_map/ppermute | solution.py:443
  159.9 4.9 %collective-permute-done.14.rc = f32[96,256]{1,0:T(8,128)S(1)} collective-permute-done((f32[96,256]{1,0:T(8,128)S(1)}, f32[96,256]{1,0:T(8,128)S(1)}, u32[]{:S(2)}, u32[]{:S(2)}) %collective-permute-start.14) | collective-permute-done | bytes 98336 | tf_op jit(solution)/shard_map/ppermute | solution.py:447
  165.8 21.1 %all_to_all.41 = f32[128,8,128]{2,1,0:T(8,128)S(1)} all-to-all(f32[128,8,128]{2,1,0:T(8,128)S(1)} %broadcast_in_dim.85), channel_id=1, replica_groups=mesh['sub'=16,'grp'=8] {'sub','grp'}, dimensions={0} | all-to-all | bytes 1048576 | tf_op jit(solution)/shard_map/all_to_all | solution.py:451
  186.9 4.5 %shard_map.114 = (f32[96,2560]{1,0:T(8,128)S(1)}, f32[96,2560]{1,0:T(8,128)S(1)}, f32[96,2560]{1,0:T(8,128)S(1)}, f32[8,128]{1,0:T(8,128)S(1)}, f32[8,128]{1,0:T(8,128)S(1)}) custom-call(f32[1024,128]{1,0:T(8,128)S(1)} %bitcast.32, bf16[48,1024]{1,0:T(8,128)(2,1)S(1)} %get-tuple-element.100.vh, bf16[48,1024]{1,0:T(8,128)(2,1)S(1)} %get-tuple-element.101.vl, ...), custom_call_target="tpu_custom_call" | custom-call | bytes 10349696 | tf_op jit(solution)/shard_map/pallas_call | solution.py:392
  191.4 17.9 %all_to_all.42 = f32[128,8,128]{2,1,0:T(8,128)S(1)} all-to-all(f32[128,8,128]{2,1,0:T(8,128)S(1)} %broadcast_in_dim.86), channel_id=1, replica_groups=mesh['sub'=16,'grp'=8] {'sub','grp'}, dimensions={0} | all-to-all | bytes 1048576 | tf_op jit(solution)/shard_map/all_to_all | solution.py:451
  209.3 4.9 %shard_map.115 = (f32[96,2560]{1,0:T(8,128)S(1)}, bf16[96,2560]{1,0:T(8,128)(2,1)S(1)}, f32[56,128]{1,0:T(8,128)S(1)}, f32[56,128]{1,0:T(8,128)S(1)}, f32[8,128]...) custom-call(f32[1024,128]{1,0:T(8,128)S(1)} %bitcast.37, bf16[48,1024]{1,0:T(8,128)(2,1)S(1)} %get-tuple-element.100.vh, ...), custom_call_target="tpu_custom_call" | custom-call | flops 503316480 | bytes 11046912 | tf_op jit(solution)/shard_map/pallas_call | solution.py:407
  214.3 5.3 %shard_map.116 = (f32[96,512]{1,0:T(8,128)S(1)}, f32[96,512]{1,0:T(8,128)S(1)}, f32[96,256]{1,0:T(8,128)S(1)}, f32[96,256]{1,0:T(8,128)S(1)}) custom-call(bf16[96,2560]{1,0:T(8,128)(2,1)S(1)} %get-tuple-element.151.p, bf16[512,512]{1,0:T(8,128)(2,1)S(1)} %get-tuple-element.111.a_g, bf16[256,256]{1,0:T(8,128)(2,1)S(1)} %get-tuple-element.112.a_c, ...), custom_call_target="tpu_custom_call" | custom-call | flops 754974720 | bytes 9011200 | tf_op jit(solution)/shard_map/pallas_call | solution.py:407
  219.5 3.1 collective-permute-start.18
  222.7 1.3 collective-permute-start.17
  224.0 1.3 collective-permute-start.16
  225.3 4.0 %collective-permute-start.15 = (f32[96,512]{1,0:T(8,128)S(1)}, f32[96,512]{1,0:T(8,128)S(1)}, u32[]{:S(2)}, u32[]{:S(2)}) collective-permute-start(f32[96,512]{1,0:T(8,128)S(1)} %get-tuple-element.150.z1), channel_id=1, source_target_pairs={{0,8},{8,16},{16,24},{24,32},{32,40},{40,48},{48,56},{56,64},{64,7... | collective-permute-start | bytes 589832 | tf_op jit(solution)/shard_map/ppermute | solution.py:443
  229.4 4.9 %collective-permute-done.19.rc = f32[96,256]{1,0:T(8,128)S(1)} collective-permute-done((f32[96,256]{1,0:T(8,128)S(1)}, f32[96,256]{1,0:T(8,128)S(1)}, u32[]{:S(2)}, u32[]{:S(2)}) %collective-permute-start.19) | collective-permute-done | bytes 98336 | tf_op jit(solution)/shard_map/ppermute | solution.py:447
  235.3 21.1 %all_to_all.43 = f32[128,8,128]{2,1,0:T(8,128)S(1)} all-to-all(f32[128,8,128]{2,1,0:T(8,128)S(1)} %broadcast_in_dim.87), channel_id=1, replica_groups=mesh['sub'=16,'grp'=8] {'sub','grp'}, dimensions={0} | all-to-all | bytes 1048576 | tf_op jit(solution)/shard_map/all_to_all | solution.py:451
  256.4 4.5 %shard_map.118 = (f32[96,2560]{1,0:T(8,128)S(1)}, f32[96,2560]{1,0:T(8,128)S(1)}, f32[96,2560]{1,0:T(8,128)S(1)}, f32[8,128]{1,0:T(8,128)S(1)}, f32[8,128]{1,0:T(8,128)S(1)}) custom-call(f32[1024,128]{1,0:T(8,128)S(1)} %bitcast.31, bf16[48,1024]{1,0:T(8,128)(2,1)S(1)} %get-tuple-element.100.vh, bf16[48,1024]{1,0:T(8,128)(2,1)S(1)} %get-tuple-element.101.vl, ...), custom_call_target="tpu_custom_call" | custom-call | bytes 10349696 | tf_op jit(solution)/shard_map/pallas_call | solution.py:392
  260.9 17.9 %all_to_all.44 = f32[128,8,128]{2,1,0:T(8,128)S(1)} all-to-all(f32[128,8,128]{2,1,0:T(8,128)S(1)} %broadcast_in_dim.88), channel_id=1, replica_groups=mesh['sub'=16,'grp'=8] {'sub','grp'}, dimensions={0} | all-to-all | bytes 1048576 | tf_op jit(solution)/shard_map/all_to_all | solution.py:451
  278.8 4.9 %shard_map.119 = (f32[96,2560]{1,0:T(8,128)S(1)}, bf16[96,2560]{1,0:T(8,128)(2,1)S(1)}, f32[56,128]{1,0:T(8,128)S(1)}, f32[56,128]{1,0:T(8,128)S(1)}, f32[8,128]...) custom-call(f32[1024,128]{1,0:T(8,128)S(1)} %bitcast.36, bf16[48,1024]{1,0:T(8,128)(2,1)S(1)} %get-tuple-element.100.vh, ...), custom_call_target="tpu_custom_call" | custom-call | flops 503316480 | bytes 11046912 | tf_op jit(solution)/shard_map/pallas_call | solution.py:407
  283.7 4.9 %shard_map.120 = (f32[96,512]{1,0:T(8,128)S(1)}, f32[96,512]{1,0:T(8,128)S(1)}, f32[96,256]{1,0:T(8,128)S(1)}, f32[96,256]{1,0:T(8,128)S(1)}) custom-call(bf16[96,2560]{1,0:T(8,128)(2,1)S(1)} %get-tuple-element.169.p, bf16[512,512]{1,0:T(8,128)(2,1)S(1)} %get-tuple-element.111.a_g, bf16[256,256]{1,0:T(8,128)(2,1)S(1)} %get-tuple-element.112.a_c, ...), custom_call_target="tpu_custom_call" | custom-call | flops 754974720 | bytes 9011200 | tf_op jit(solution)/shard_map/pallas_call | solution.py:407
  288.6 3.1 collective-permute-start.23
  291.8 1.3 collective-permute-start.22
  294.4 4.0 %collective-permute-start.20 = (f32[96,512]{1,0:T(8,128)S(1)}, f32[96,512]{1,0:T(8,128)S(1)}, u32[]{:S(2)}, u32[]{:S(2)}) collective-permute-start(f32[96,512]{1,0:T(8,128)S(1)} %get-tuple-element.168.z1), channel_id=1, source_target_pairs={{0,8},{8,16},{16,24},{24,32},{32,40},{40,48},{48,56},{56,64},{64,7... | collective-permute-start | bytes 589832 | tf_op jit(solution)/shard_map/ppermute | solution.py:443
  298.6 4.9 %collective-permute-done.24.rc = f32[96,256]{1,0:T(8,128)S(1)} collective-permute-done((f32[96,256]{1,0:T(8,128)S(1)}, f32[96,256]{1,0:T(8,128)S(1)}, u32[]{:S(2)}, u32[]{:S(2)}) %collective-permute-start.24) | collective-permute-done | bytes 98336 | tf_op jit(solution)/shard_map/ppermute | solution.py:447
  304.4 21.1 %all_to_all.45 = f32[128,8,128]{2,1,0:T(8,128)S(1)} all-to-all(f32[128,8,128]{2,1,0:T(8,128)S(1)} %broadcast_in_dim.89), channel_id=1, replica_groups=mesh['sub'=16,'grp'=8] {'sub','grp'}, dimensions={0} | all-to-all | bytes 1048576 | tf_op jit(solution)/shard_map/all_to_all | solution.py:451
  325.5 4.5 %shard_map.122 = (f32[96,2560]{1,0:T(8,128)}, f32[96,2560]{1,0:T(8,128)}) custom-call(f32[1024,128]{1,0:T(8,128)S(1)} %bitcast.34, bf16[48,1024]{1,0:T(8,128)(2,1)S(1)} %get-tuple-element.100.vh, bf16[48,1024]{1,0:T(8,128)(2,1)S(1)} %get-tuple-element.101.vl, s32[8,128]{1,0:T(8,128)S(1)} %pad.24.codes.codes_rows, f32[8,128]{1,0:T(8,128)S(1)} %get-tuple-element.178.scal, ...), custom_call_target="tpu_custom_call" | custom-call | bytes 9117696 | tf_op jit(solution)/shard_map/pallas_call | solution.py:392
  (129 shorter events, 31.1 us)
Async XLA Ops:
  8.3 44.8 %copy-start.6 = (bf16[512,512]{1,0:T(8,128)(2,1)}, bf16[512,512]{1,0:T(8,128)(2,1)S(1)}, u32[]{:S(2)}) copy-start(bf16[512,512]{1,0:T(8,128)(2,1)S(1)} %get-tuple-element.106.at_g) | copy-start | bytes 1572868
  8.3 49.0 %copy-start.15 = (bf16[256,256]{1,0:T(8,128)(2,1)}, bf16[256,256]{1,0:T(8,128)(2,1)S(1)}, u32[]{:S(2)}) copy-start(bf16[256,256]{1,0:T(8,128)(2,1)S(1)} %get-tuple-element.107.at_c) | copy-start | bytes 393220
  8.3 53.9 %copy-start.4 = (bf16[512,512]{1,0:T(8,128)(2,1)}, bf16[512,512]{1,0:T(8,128)(2,1)S(1)}, u32[]{:S(2)}) copy-start(bf16[512,512]{1,0:T(8,128)(2,1)S(1)} %get-tuple-element.105.at_s) | copy-start | bytes 1572868
  8.3 54.0 %copy-start.1 = (bf16[512,512]{1,0:T(8,128)(2,1)}, bf16[512,512]{1,0:T(8,128)(2,1)S(1)}, u32[]{:S(2)}) copy-start(bf16[512,512]{1,0:T(8,128)(2,1)S(1)} %get-tuple-element.104.a_s) | copy-start | bytes 1572868
  8.3 15.9 %collective-permute-start = (f32[32,512]{1,0:T(8,128)S(1)}, f32[32,512]{1,0:T(8,128)S(1)}, u32[]{:S(2)}, u32[]{:S(2)}) collective-permute-start(f32[32,512]{1,0:T(8,128)S(1)} %get-tuple-element.94), channel_id=1, source_target_pairs={{0,8},{8,16},{16,24},{24,32},{32,40},{40,48},{48,56},{56,64},{64,7... | collective-permute-start | bytes 196616 | tf_op jit(solution)/shard_map/ppermute | solution.py:443
  12.3 11.9 %collective-permute-start.1 = (f32[32,512]{1,0:T(8,128)S(1)}, f32[32,512]{1,0:T(8,128)S(1)}, u32[]{:S(2)}, u32[]{:S(2)}) collective-permute-start(f32[32,512]{1,0:T(8,128)S(1)} %get-tuple-element.95), channel_id=1, source_target_pairs={{8,0},{16,8},{24,16},{32,24},{40,32},{48,40},{56,48},{64,56},{72,6... | collective-permute-start | bytes 196616 | tf_op jit(solution)/shard_map/ppermute | solution.py:444
  13.6 10.6 %collective-permute-start.2 = (f32[32,512]{1,0:T(8,128)S(1)}, f32[32,512]{1,0:T(8,128)S(1)}, u32[]{:S(2)}, u32[]{:S(2)}) collective-permute-start(f32[32,512]{1,0:T(8,128)S(1)} %get-tuple-element.96), channel_id=1, source_target_pairs={{0,1},{2,3},{3,4},{4,5},{6,7},{8,9},{10,11},{11,12},{12,13},{14,15... | collective-permute-start | bytes 196616 | tf_op jit(solution)/shard_map/ppermute | solution.py:445
  14.9 9.3 %collective-permute-start.3 = (f32[32,512]{1,0:T(8,128)S(1)}, f32[32,512]{1,0:T(8,128)S(1)}, u32[]{:S(2)}, u32[]{:S(2)}) collective-permute-start(f32[32,512]{1,0:T(8,128)S(1)} %get-tuple-element.97), channel_id=1, source_target_pairs={{1,0},{3,2},{4,3},{5,4},{7,6},{9,8},{11,10},{12,11},{13,12},{15,14... | collective-permute-start | bytes 196616 | tf_op jit(solution)/shard_map/ppermute | solution.py:446
  17.9 6.3 %collective-permute-start.4 = (f32[48,256]{1,0:T(8,128)S(1)}, f32[48,256]{1,0:T(8,128)S(1)}, u32[]{:S(2)}, u32[]{:S(2)}) collective-permute-start(f32[48,256]{1,0:T(8,128)S(1)} %get-tuple-element.98), channel_id=1, source_target_pairs={{0,4},{1,5},{2,6},{3,7},{4,0},{5,1},{6,2},{7,3},{8,12},{9,13},{10,... | collective-permute-start | bytes 147464 | tf_op jit(solution)/shard_map/ppermute | solution.py:447
  26.0 36.3 %copy-start = (bf16[256,2560]{1,0:T(8,128)(2,1)}, bf16[256,2560]{1,0:T(8,128)(2,1)S(1)}, u32[]{:S(2)}) copy-start(bf16[256,2560]{1,0:T(8,128)(2,1)S(1)} %get-tuple-element.103.t_stack) | copy-start | bytes 3932164
  26.0 36.3 %copy-start.8 = (f32[96,2560]{1,0:T(8,128)}, f32[96,2560]{1,0:T(8,128)S(1)}, u32[]{:S(2)}) copy-start(f32[96,2560]{1,0:T(8,128)S(1)} %get-tuple-element.102.u.point) | copy-start | bytes 2949124
  53.1 9.2 %copy-start.21 = (f32[1,96,2560]{2,1,0:T(8,128)S(1)}, f32[1,96,2560]{2,1,0:T(8,128)}, u32[]{:S(2)}) copy-start(f32[1,96,2560]{2,1,0:T(8,128)} %param.13) | copy-start | bytes 2949124
  57.4 18.7 %copy-start.32 = (s32[96,3]{0,1:T(4,128)S(1)}, s32[96,3]{0,1:T(4,128)}, u32[]{:S(2)}) copy-start(s32[96,3]{0,1:T(4,128)} %param.17) | copy-start | bytes 3460
  62.3 72.6 %copy-start.5 = (bf16[512,512]{1,0:T(8,128)(2,1)S(1)}, bf16[512,512]{1,0:T(8,128)(2,1)}, u32[]{:S(2)}) copy-start(bf16[512,512]{1,0:T(8,128)(2,1)} %copy-done.4) | copy-start | bytes 1572868
  64.4 16.8 %collective-permute-start.6 = (f32[96,512]{1,0:T(8,128)S(1)}, f32[96,512]{1,0:T(8,128)}, u32[]{:S(2)}, u32[]{:S(2)}) collective-permute-start(f32[96,512]{1,0:T(8,128)S(1)} %get-tuple-element.117.z0), channel_id=1, source_target_pairs={{8,0},{16,8},{24,16},{32,24},{40,32},{48,40},{56,48},{64,56},{72,6... | collective-permute-start | bytes 589832 | tf_op jit(solution)/shard_map/ppermute | solution.py:444
  65.7 15.5 %collective-permute-start.5 = (f32[96,512]{1,0:T(8,128)S(1)}, f32[96,512]{1,0:T(8,128)}, u32[]{:S(2)}, u32[]{:S(2)}) collective-permute-start(f32[96,512]{1,0:T(8,128)S(1)} %get-tuple-element.118.z1), channel_id=1, source_target_pairs={{0,8},{8,16},{16,24},{24,32},{32,40},{40,48},{48,56},{56,64},{64,7... | collective-permute-start | bytes 589832 | tf_op jit(solution)/shard_map/ppermute | solution.py:443
  70.4 10.9 %collective-permute-start.8 = (f32[96,512]{1,0:T(8,128)S(1)}, f32[96,512]{1,0:T(8,128)}, u32[]{:S(2)}, u32[]{:S(2)}) collective-permute-start(f32[96,512]{1,0:T(8,128)S(1)} %get-tuple-element.119.z2), channel_id=1, source_target_pairs={{1,0},{3,2},{4,3},{5,4},{7,6},{9,8},{11,10},{12,11},{13,12},{15,14... | collective-permute-start | bytes 589832 | tf_op jit(solution)/shard_map/ppermute | solution.py:446
  74.7 6.5 %collective-permute-start.7 = (f32[96,512]{1,0:T(8,128)}, f32[96,512]{1,0:T(8,128)}, u32[]{:S(2)}, u32[]{:S(2)}) collective-permute-start(f32[96,512]{1,0:T(8,128)} %get-tuple-element.120.z3), channel_id=1, source_target_pairs={{0,1},{2,3},{3,4},{4,5},{6,7},{8,9},{10,11},{11,12},{12,13},{14,15... | collective-permute-start | bytes 589832 | tf_op jit(solution)/shard_map/ppermute | solution.py:445
  76.2 5.0 %collective-permute-start.9 = (f32[96,256]{1,0:T(8,128)S(1)}, f32[96,256]{1,0:T(8,128)S(1)}, u32[]{:S(2)}, u32[]{:S(2)}) collective-permute-start(f32[96,256]{1,0:T(8,128)S(1)} %get-tuple-element.121.zc), channel_id=1, source_target_pairs={{0,4},{1,5},{2,6},{3,7},{4,0},{5,1},{6,2},{7,3},{8,12},{9,13},{10,... | collective-permute-start | bytes 294920 | tf_op jit(solution)/shard_map/ppermute | solution.py:447
  85.8 20.4 %all-to-all-start.1 = ((f32[128,8,128]{2,1,0:T(8,128)}), f32[128,8,128]{2,1,0:T(8,128)S(1)}, u32[]{:S(2)}, u32[]{:S(2)}) async-start(f32[128,8,128]{2,1,0:T(8,128)} %broadcast_in_dim.34), calls=%async_computation.1 | async-start | bytes 1048576 | tf_op jit(solution)/shard_map/all_to_all | solution.py:451
  106.2 1.2 copy-start.9
  107.4 1.2 copy-start.20
  115.6 18.5 %all-to-all-start.2 = ((f32[128,8,128]{2,1,0:T(8,128)}), f32[128,8,128]{2,1,0:T(8,128)S(1)}, u32[]{:S(2)}, u32[]{:S(2)}) async-start(f32[128,8,128]{2,1,0:T(8,128)} %broadcast_in_dim.82), calls=%async_computation.2 | async-start | bytes 1048576 | tf_op jit(solution)/shard_map/all_to_all | solution.py:451
  134.9 1.0 copy-start.2
  137.0 1.2 copy-start.14
  144.7 42.2 %copy-start.12 = (f32[96,2560]{1,0:T(8,128)}, f32[96,2560]{1,0:T(8,128)S(1)}, u32[]{:S(2)}) copy-start(f32[96,2560]{1,0:T(8,128)S(1)} %get-tuple-element.139.q.d) | copy-start | bytes 2949124
  144.7 42.1 %copy-start.10 = (f32[96,2560]{1,0:T(8,128)S(1)}, f32[96,2560]{1,0:T(8,128)}, u32[]{:S(2)}) copy-start(f32[96,2560]{1,0:T(8,128)} %copy-done.8) | copy-start | bytes 2949124
  144.7 42.1 %copy-start.28 = (f32[96,256]{1,0:T(8,128)S(1)}, f32[96,256]{1,0:T(8,128)}, u32[]{:S(2)}) copy-start(f32[96,256]{1,0:T(8,128)} %copy-done.26) | copy-start | bytes 294916
  144.7 64.6 %copy-start.3 = (bf16[512,512]{1,0:T(8,128)(2,1)S(1)}, bf16[512,512]{1,0:T(8,128)(2,1)}, u32[]{:S(2)}) copy-start(bf16[512,512]{1,0:T(8,128)(2,1)} %copy-done.1) | copy-start | bytes 1572868
  150.0 14.8 %collective-permute-start.13 = (f32[96,512]{1,0:T(8,128)S(1)}, f32[96,512]{1,0:T(8,128)S(1)}, u32[]{:S(2)}, u32[]{:S(2)}) collective-permute-start(f32[96,512]{1,0:T(8,128)S(1)} %get-tuple-element.135.z2), channel_id=1, source_target_pairs={{1,0},{3,2},{4,3},{5,4},{7,6},{9,8},{11,10},{12,11},{13,12},{15,14... | collective-permute-start | bytes 589832 | tf_op jit(solution)/shard_map/ppermute | solution.py:446
  153.2 11.7 %collective-permute-start.12 = (f32[96,512]{1,0:T(8,128)S(1)}, f32[96,512]{1,0:T(8,128)S(1)}, u32[]{:S(2)}, u32[]{:S(2)}) collective-permute-start(f32[96,512]{1,0:T(8,128)S(1)} %get-tuple-element.136.z3), channel_id=1, source_target_pairs={{0,1},{2,3},{3,4},{4,5},{6,7},{8,9},{10,11},{11,12},{12,13},{14,15... | collective-permute-start | bytes 589832 | tf_op jit(solution)/shard_map/ppermute | solution.py:445
  154.5 10.4 %collective-permute-start.11 = (f32[96,512]{1,0:T(8,128)S(1)}, f32[96,512]{1,0:T(8,128)S(1)}, u32[]{:S(2)}, u32[]{:S(2)}) collective-permute-start(f32[96,512]{1,0:T(8,128)S(1)} %get-tuple-element.132.z0), channel_id=1, source_target_pairs={{8,0},{16,8},{24,16},{32,24},{40,32},{48,40},{56,48},{64,56},{72,6... | collective-permute-start | bytes 589832 | tf_op jit(solution)/shard_map/ppermute | solution.py:444
  155.8 9.1 %collective-permute-start.10 = (f32[96,512]{1,0:T(8,128)S(1)}, f32[96,512]{1,0:T(8,128)S(1)}, u32[]{:S(2)}, u32[]{:S(2)}) collective-permute-start(f32[96,512]{1,0:T(8,128)S(1)} %get-tuple-element.133.z1), channel_id=1, source_target_pairs={{0,8},{8,16},{16,24},{24,32},{32,40},{40,48},{48,56},{56,64},{64,7... | collective-permute-start | bytes 589832 | tf_op jit(solution)/shard_map/ppermute | solution.py:443
  159.8 5.1 %collective-permute-start.14 = (f32[96,256]{1,0:T(8,128)S(1)}, f32[96,256]{1,0:T(8,128)S(1)}, u32[]{:S(2)}, u32[]{:S(2)}) collective-permute-start(f32[96,256]{1,0:T(8,128)S(1)} %get-tuple-element.137.zc), channel_id=1, source_target_pairs={{0,4},{1,5},{2,6},{3,7},{4,0},{5,1},{6,2},{7,3},{8,12},{9,13},{10,... | collective-permute-start | bytes 294920 | tf_op jit(solution)/shard_map/ppermute | solution.py:447
  165.7 21.1 %copy-start.25 = (f32[96,2560]{1,0:T(8,128)}, f32[96,2560]{1,0:T(8,128)S(1)}, u32[]{:S(2)}) copy-start(f32[96,2560]{1,0:T(8,128)S(1)} %get-tuple-element.145.image) | copy-start | bytes 2949124
  191.3 28.2 %copy-start.23 = (f32[96,2560]{1,0:T(8,128)}, f32[96,2560]{1,0:T(8,128)S(1)}, u32[]{:S(2)}) copy-start(f32[96,2560]{1,0:T(8,128)S(1)} %get-tuple-element.162.gradient) | copy-start | bytes 2949124
  214.2 42.1 %copy-start.11 = (f32[96,2560]{1,0:T(8,128)}, f32[96,2560]{1,0:T(8,128)S(1)}, u32[]{:S(2)}) copy-start(f32[96,2560]{1,0:T(8,128)S(1)} %get-tuple-element.156.q.d) | copy-start | bytes 2949124
  219.5 14.8 %collective-permute-start.18 = (f32[96,512]{1,0:T(8,128)S(1)}, f32[96,512]{1,0:T(8,128)S(1)}, u32[]{:S(2)}, u32[]{:S(2)}) collective-permute-start(f32[96,512]{1,0:T(8,128)S(1)} %get-tuple-element.152.z2), channel_id=1, source_target_pairs={{1,0},{3,2},{4,3},{5,4},{7,6},{9,8},{11,10},{12,11},{13,12},{15,14... | collective-permute-start | bytes 589832 | tf_op jit(solution)/shard_map/ppermute | solution.py:446
  222.7 11.7 %collective-permute-start.17 = (f32[96,512]{1,0:T(8,128)S(1)}, f32[96,512]{1,0:T(8,128)S(1)}, u32[]{:S(2)}, u32[]{:S(2)}) collective-permute-start(f32[96,512]{1,0:T(8,128)S(1)} %get-tuple-element.153.z3), channel_id=1, source_target_pairs={{0,1},{2,3},{3,4},{4,5},{6,7},{8,9},{10,11},{11,12},{12,13},{14,15... | collective-permute-start | bytes 589832 | tf_op jit(solution)/shard_map/ppermute | solution.py:445
  224.0 10.4 %collective-permute-start.16 = (f32[96,512]{1,0:T(8,128)S(1)}, f32[96,512]{1,0:T(8,128)S(1)}, u32[]{:S(2)}, u32[]{:S(2)}) collective-permute-start(f32[96,512]{1,0:T(8,128)S(1)} %get-tuple-element.149.z0), channel_id=1, source_target_pairs={{8,0},{16,8},{24,16},{32,24},{40,32},{48,40},{56,48},{64,56},{72,6... | collective-permute-start | bytes 589832 | tf_op jit(solution)/shard_map/ppermute | solution.py:444
  225.3 9.1 %collective-permute-start.15 = (f32[96,512]{1,0:T(8,128)S(1)}, f32[96,512]{1,0:T(8,128)S(1)}, u32[]{:S(2)}, u32[]{:S(2)}) collective-permute-start(f32[96,512]{1,0:T(8,128)S(1)} %get-tuple-element.150.z1), channel_id=1, source_target_pairs={{0,8},{8,16},{16,24},{24,32},{32,40},{40,48},{48,56},{56,64},{64,7... | collective-permute-start | bytes 589832 | tf_op jit(solution)/shard_map/ppermute | solution.py:443
  229.3 5.1 %collective-permute-start.19 = (f32[96,256]{1,0:T(8,128)S(1)}, f32[96,256]{1,0:T(8,128)S(1)}, u32[]{:S(2)}, u32[]{:S(2)}) collective-permute-start(f32[96,256]{1,0:T(8,128)S(1)} %get-tuple-element.154.zc), channel_id=1, source_target_pairs={{0,4},{1,5},{2,6},{3,7},{4,0},{5,1},{6,2},{7,3},{8,12},{9,13},{10,... | collective-permute-start | bytes 294920 | tf_op jit(solution)/shard_map/ppermute | solution.py:447
  235.2 21.1 %copy-start.24 = (f32[96,2560]{1,0:T(8,128)}, f32[96,2560]{1,0:T(8,128)S(1)}, u32[]{:S(2)}) copy-start(f32[96,2560]{1,0:T(8,128)S(1)} %get-tuple-element.163.image) | copy-start | bytes 2949124
  288.6 14.8 %collective-permute-start.23 = (f32[96,512]{1,0:T(8,128)S(1)}, f32[96,512]{1,0:T(8,128)S(1)}, u32[]{:S(2)}, u32[]{:S(2)}) collective-permute-start(f32[96,512]{1,0:T(8,128)S(1)} %get-tuple-element.170.z2), channel_id=1, source_target_pairs={{1,0},{3,2},{4,3},{5,4},{7,6},{9,8},{11,10},{12,11},{13,12},{15,14... | collective-permute-start | bytes 589832 | tf_op jit(solution)/shard_map/ppermute | solution.py:446
  291.8 11.7 %collective-permute-start.22 = (f32[96,512]{1,0:T(8,128)S(1)}, f32[96,512]{1,0:T(8,128)S(1)}, u32[]{:S(2)}, u32[]{:S(2)}) collective-permute-start(f32[96,512]{1,0:T(8,128)S(1)} %get-tuple-element.171.z3), channel_id=1, source_target_pairs={{0,1},{2,3},{3,4},{4,5},{6,7},{8,9},{10,11},{11,12},{12,13},{14,15... | collective-permute-start | bytes 589832 | tf_op jit(solution)/shard_map/ppermute | solution.py:445
  293.1 10.4 %collective-permute-start.21 = (f32[96,512]{1,0:T(8,128)S(1)}, f32[96,512]{1,0:T(8,128)S(1)}, u32[]{:S(2)}, u32[]{:S(2)}) collective-permute-start(f32[96,512]{1,0:T(8,128)S(1)} %get-tuple-element.167.z0), channel_id=1, source_target_pairs={{8,0},{16,8},{24,16},{32,24},{40,32},{48,40},{56,48},{64,56},{72,6... | collective-permute-start | bytes 589832 | tf_op jit(solution)/shard_map/ppermute | solution.py:444
  294.4 9.1 %collective-permute-start.20 = (f32[96,512]{1,0:T(8,128)S(1)}, f32[96,512]{1,0:T(8,128)S(1)}, u32[]{:S(2)}, u32[]{:S(2)}) collective-permute-start(f32[96,512]{1,0:T(8,128)S(1)} %get-tuple-element.168.z1), channel_id=1, source_target_pairs={{0,8},{8,16},{16,24},{24,32},{32,40},{40,48},{48,56},{56,64},{64,7... | collective-permute-start | bytes 589832 | tf_op jit(solution)/shard_map/ppermute | solution.py:443
  298.4 5.1 %collective-permute-start.24 = (f32[96,256]{1,0:T(8,128)S(1)}, f32[96,256]{1,0:T(8,128)S(1)}, u32[]{:S(2)}, u32[]{:S(2)}) collective-permute-start(f32[96,256]{1,0:T(8,128)S(1)} %get-tuple-element.172.zc), channel_id=1, source_target_pairs={{0,4},{1,5},{2,6},{3,7},{4,0},{5,1},{6,2},{7,3},{8,12},{9,13},{10,... | collective-permute-start | bytes 294920 | tf_op jit(solution)/shard_map/ppermute | solution.py:447
  (12 other events, 10.6 us)

commit v2 on v1

v2 whole, which is shorter than its diff:
```python
import functools

import jax
import jax.numpy as jnp
from jax import lax
from jax.experimental import pallas as pl
from jax.experimental.pallas import tpu as pltpu
from jax.sharding import PartitionSpec as P

FACE = 512
CONT = 256
ORDER = 2560
MODES = 6
NLOAD = 96
ITERS = 3
CON = 4 * FACE
SEGS = ((0, 512), (512, 512), (1024, 512), (1536, 512), (2048, 256), (2304, 256))

F32 = jnp.float32
BF16 = jnp.bfloat16
step_scale = 0.2
AXES = ("sub", "grp")


def sds(shape, dtype=F32):
    return jax.ShapeDtypeStruct(shape, dtype)


def mm(a, b):
    return jnp.dot(a, b, preferred_element_type=F32)


def split2(x):
    hi = x.astype(BF16)
    return hi, (x - hi.astype(F32)).astype(BF16)


def turned(x, order):
    return lax.dot_general(x, order, (((1,), (1,)), ((), ())), preferred_element_type=F32)


def parts3(x):
    hi = x.astype(BF16)
    rest = x - hi.astype(F32)
    mid = rest.astype(BF16)
    return hi, mid, (rest - mid.astype(F32)).astype(BF16)


def shuffle(x, order):
    return sum(turned(part, order) for part in parts3(x))


def shuffle_back(x, order):
    return sum(mm(part, order) for part in parts3(x))


def flip(x):
    rows = x.shape[0]
    if rows % 128:
        x = jnp.concatenate([x, jnp.zeros((128 - rows % 128, x.shape[1]), F32)], axis=0)
    return x.T


def cut(width):
    return [(at, min(width, ORDER - at)) for at in range(0, ORDER, width)]


def spread(rows):
    hi = rows.astype(BF16).astype(F32)
    stack = jnp.concatenate([hi, hi, rows - hi, jnp.zeros((112, 128), F32)], axis=0)
    return stack.T[:NLOAD].astype(BF16)


def coarse(vh, vl, g):
    gh, gl = split2(g)
    return mm(vh, gh) + mm(vl, gh) + mm(vh, gl)


def project_rows(x, bh, bl):
    xh, xl = split2(x)
    return mm(xh, bh) + mm(xl, bh) + mm(xh, bl)


def lanesum(x):
    return jnp.sum(x, axis=1, keepdims=True)


def message(coef_t, first, second):
    lane = lax.broadcasted_iota(jnp.int32, coef_t.shape, 1)
    full = jnp.where(lane == 6, first, jnp.where(lane == 7, second, coef_t))
    return flip(full)[:8]


def send_faces(par, faces, refs):
    even_i, even_j = par[0:1, :] > 0.5, par[1:2, :] > 0.5
    f0, f1, f2, f3 = faces
    refs[0][...] = jnp.where(even_i, f1, f0)
    refs[1][...] = jnp.where(even_i, f0, f1)
    refs[2][...] = jnp.where(even_j, f3, f2)
    refs[3][...] = jnp.where(even_j, f2, f3)


def take_faces(par, refs):
    even_i, even_j = par[0:1, :] > 0.5, par[1:2, :] > 0.5
    xa, xb, ya, yb = (ref[...] for ref in refs)
    return (
        jnp.where(even_i, xb, xa),
        jnp.where(even_i, xa, xb),
        jnp.where(even_j, yb, ya),
        jnp.where(even_j, ya, yb),
    )


def weight(par, at):
    if at < CON:
        row = 2 + at // FACE
        return par[row : row + 1, :]
    return 0.5 if at == CON else 1.0


def padded(x, rows, columns):
    if x.shape[1] < columns:
        x = jnp.concatenate([x, jnp.zeros((x.shape[0], columns - x.shape[1]), F32)], axis=1)
    if x.shape[0] < rows:
        x = jnp.concatenate([x, jnp.zeros((rows - x.shape[0], columns), F32)], axis=0)
    return x


def prepare_kernel(
    basis, vp, coeff, face_rows, contact_row, flags, codes, par,
    o_s, o_g, o_c, basis_out, coeff_out, act_out, code_columns, code_rows, xa, xb, ya, yb, mc,
):
    for row, out in ((face_rows[0:1, :], o_s), (face_rows[1:2, :], o_g), (contact_row[...], o_c)):
        n = row.shape[1]
        out[...] = (lax.broadcasted_iota(jnp.int32, (n, n), 0) == row).astype(F32).astype(BF16)
    rows = padded(basis[...], 8, ORDER)
    parts = [
        rows[:, 0:512],
        shuffle(rows[:, 512:1024], o_s[...]),
        rows[:, 1024:1536],
        shuffle(rows[:, 1536:2048], o_g[...]),
        shuffle(rows[:, 2048:2304], o_c[...]),
        rows[:, 2304:2560],
    ]
    for (at, width), part in zip(SEGS, parts):
        basis_out[:, at : at + width] = part
    act_out[...] = turned(flags[...].astype(F32).astype(BF16), o_c[...])
    code = padded(codes[...].astype(F32), NLOAD, 128)
    code_columns[...] = code
    code_rows[...] = flip(code)[:8]
    inv = vp[...]
    own = padded(coeff[...], 8, 512)
    coeff_out[...] = own[:, :128]
    extra = [inv[:, 0:512], inv[:, 512:1024], own]
    send_faces(
        par,
        [jnp.concatenate([part] + extra, axis=0) for part in parts[:4]],
        (xa, xb, ya, yb),
    )
    mc[0:8, :] = parts[4]
    for k in range(4):
        mc[8 + 8 * k : 16 + 8 * k, :] = inv[:, 256 * k : 256 * k + 256]
    mc[40:48, :] = own[:, :256]


def start_kernel(
    basis, vp, coeff, par, columns, xa, xb, ya, yb, rc,
    t_stack, vh, vl, bh, bl, point, msg,
):
    zero8 = jnp.zeros((8, ORDER), F32)
    pieces = [basis[...]]
    rows = [vp[...]]
    coefs = [coeff[...]]
    for k, got in enumerate(take_faces(par, (xa, xb, ya, yb))):
        at = FACE * k
        left = [zero8[:, :at]] if at else []
        pieces.append(jnp.concatenate(left + [got[0:8, :], zero8[:, at + FACE :]], axis=1))
        rows.append(jnp.concatenate([got[8:16, :], got[16:24, :]], axis=1))
        coefs.append(got[24:32, 0:128])
    pieces.append(jnp.concatenate([zero8[:, :CON], rc[0:8, :], zero8[:, CON + CONT :]], axis=1))
    rows.append(jnp.concatenate([rc[8 + 8 * k : 16 + 8 * k, :] for k in range(4)], axis=1))
    coefs.append(rc[40:48, 0:128])
    th, tl = split2(jnp.concatenate(pieces, axis=0))
    t_stack[0:48, :] = th
    t_stack[48:96, :] = tl
    t_stack[96:144, :] = th
    t_stack[144:256, :] = jnp.zeros((112, ORDER), BF16)
    hi, low = split2(jnp.concatenate(rows, axis=0))
    vh[...] = hi
    vl[...] = low
    bhi, blow = split2(flip(basis[...]))
    bh[...] = bhi
    bl[...] = blow
    factor = spread(jnp.concatenate(coefs, axis=0))
    coef_t = jnp.zeros((NLOAD, 128), F32)
    for at, width in SEGS:
        seg = slice(at, at + width)
        x = mm(factor, t_stack[:, seg])
        if at == CON:
            x = jnp.maximum(x, 0.0)
        point[:, seg] = x
        coef_t += project_rows(x, bh[seg, :], bl[seg, :])
    msg[...] = columns[...] + flip(coef_t)[:8][None]


def rounded(x, at, orders):
    x = x.astype(BF16)
    order = dict(zip((512, 1536, 2048), orders)).get(at)
    return x if order is None else mm(x, order[...]).astype(BF16)


def product_block(p, schur, orders, z, load=None):
    step = pl.program_id(0)
    y = mm(p[...], schur[...])
    if load is not None:
        y = y - load[...]
    for n in range(5):

        @pl.when(step == n)
        def _():
            x = y
            if n == 4:
                x = jnp.concatenate([shuffle(x[:, :CONT], orders[2][...]), x[:, CONT:]], axis=1)
            elif n in (1, 3):
                x = shuffle(x, orders[n // 2][...])
            z[:, FACE * n : FACE * (n + 1)] = x


def send_product(par, z, xa, xb, ya, yb, xc):
    @pl.when(pl.program_id(0) == 4)
    def _():
        send_faces(par, [z[:, FACE * n : FACE * (n + 1)] for n in range(4)], (xa, xb, ya, yb))
        xc[...] = z[:, CON : CON + CONT]


def first_search_kernel(
    g, vh, vl, par, u, t_stack, o_s, o_g, o_c, load, schur,
    gh, gl, z, xa, xb, ya, yb, xc, p,
):
    orders = (o_s, o_g, o_c)

    @pl.when(pl.program_id(0) == 0)
    def _():
        column = flip(g[...])[96:112]
        row = lax.broadcasted_iota(jnp.int32, column.shape, 0)
        hi, low = split2(jnp.where(row < MODES, column, 0.0))
        gh[...] = hi
        gl[...] = low
        factor = spread(coarse(vh[...], vl[...], g[...]))
        for at, width in SEGS:
            seg = slice(at, at + width)
            p[:, seg] = rounded(u[:, seg] - mm(factor, t_stack[:, seg]), at, orders)

    product_block(p, schur, orders, z, load)
    send_product(par, z, xa, xb, ya, yb, xc)


def search_kernel(
    k, g, vh, vl, gh, gl, codes, scal, prev, par, u, d, t_stack, o_s, o_g, o_c, schur,
    coef_u, coef_q, scal_out, q, z, xa, xb, ya, yb, xc, p,
):
    orders = (o_s, o_g, o_c)

    @pl.when(pl.program_id(0) == 0)
    def _():
        got = g[...]
        gah, gal = split2(got)
        alpha = mm(vh[...], gah) + mm(vl[...], gah) + mm(vh[...], gal)
        gamma = (mm(gh[...], gah) + mm(gl[...], gah) + mm(gh[...], gal))[:8]
        sums = jnp.sum(got.reshape(128, 8, 128), axis=0)
        mix = jnp.concatenate([alpha, gamma], axis=0)
        coef_u[...] = mix
        scal_out[0:1, :] = sums[7:8]
        scal_out[1:8, :] = jnp.zeros((7, 128), F32)
        if k > 0:
            bend = sums[6:7]
            length, curve, cross = scal[0:1], scal[1:2], scal[2:3]
            both = (codes[k : k + 1] == 0) & (codes[k - 1 : k] == 0)
            factor2 = jnp.where(both, (cross - length * bend) / curve, 0.0)
            mix = jnp.where(factor2 == 0.0, mix, mix - factor2 * prev[...])
            g2 = flip(jnp.broadcast_to(factor2, (8, 128)))[:NLOAD, 0:1]
        coef_q[...] = mix
        factor = spread(mix[:48])
        for at, width in SEGS:
            seg = slice(at, at + width)
            x = u[:, seg]
            if k > 0:
                x = x - g2 * d[:, seg]
            q[:, seg] = x
            p[:, seg] = rounded(x - mm(factor, t_stack[:, seg]), at, orders)

    product_block(p, schur, orders, z)
    send_product(par, z, xa, xb, ya, yb, xc)


def image_kernel(
    z, xa, xb, ya, yb, rc, par, q, u, coef_u, coef_q, bh, bl,
    image, msg,
):
    coef_t = jnp.zeros((NLOAD, 128), F32)
    curve = jnp.zeros((NLOAD, 1), F32)
    cross = jnp.zeros((NLOAD, 1), F32)
    coming = take_faces(par, (xa, xb, ya, yb)) + (rc[...], None)
    for (at, width), got in zip(SEGS, coming):
        seg = slice(at, at + width)
        x = z[:, seg] if got is None else z[:, seg] + got
        image[:, seg] = x
        coef_t += project_rows(x, bh[seg, :], bl[seg, :])
        xw = x * weight(par, at)
        curve += lanesum(q[:, seg] * xw)
        cross += lanesum(u[:, seg] * xw)
    rows = message(coef_t, curve, cross)
    row = lax.broadcasted_iota(jnp.int32, (8, 128), 0)
    modes = jnp.where(row < MODES, rows, 0.0)
    fix_q = jnp.sum(coef_q[48:56] * modes, axis=0, keepdims=True)
    fix_u = jnp.sum(coef_u[48:56] * modes, axis=0, keepdims=True)
    rows = rows - jnp.where(row == 6, fix_q, 0.0) - jnp.where(row == 7, fix_u, 0.0)
    msg[...] = jnp.broadcast_to(rows[None], msg.shape)


def first_image_kernel(z, xa, xb, ya, yb, rc, par, bh, bl, image, msg):
    coef_t = jnp.zeros((NLOAD, 128), F32)
    coming = take_faces(par, (xa, xb, ya, yb)) + (rc[...], None)
    for (at, width), got in zip(SEGS, coming):
        seg = slice(at, at + width)
        x = z[:, seg] if got is None else z[:, seg] + got
        image[:, seg] = x
        coef_t += project_rows(x, bh[seg, :], bl[seg, :])
    msg[...] = jnp.broadcast_to(flip(coef_t)[:8][None], msg.shape)


def next_part(seg, at, codes, m, g, w, act, weight):
    bent = w * w
    if at == CON:
        free = 1.0 - act
        free_grad = free * g
        bent = free * bent
        chopped = act * jnp.minimum(g, 0.0)
        trial = jnp.maximum(m - step_scale * free_grad, 0.0)
    else:
        free_grad = g
        chopped = 0.0
        trial = m - step_scale * g
    u = jnp.where(codes == 0, free_grad, jnp.where(codes == 2, chopped, trial - m))
    return u, lanesum(g * u * weight), lanesum(bent * weight)


def first_update_kernel(
    g, vh, vl, codes, point, image, act, par, t_stack, bh, bl,
    gradient, u, msg,
):
    factor = spread(coarse(vh[...], vl[...], g[...]))
    code = codes[:, 0:1]
    coef_t = jnp.zeros((NLOAD, 128), F32)
    slope = jnp.zeros((NLOAD, 1), F32)
    for at, width in SEGS:
        seg = slice(at, at + width)
        grad = image[:, seg] - mm(factor, t_stack[:, seg])
        gradient[:, seg] = grad
        x, slope_part, _ = next_part(seg, at, code, point[:, seg], grad, grad, act[...], weight(par, at))
        u[:, seg] = x
        slope += slope_part
        coef_t += project_rows(x, bh[seg, :], bl[seg, :])
    rows = message(coef_t, jnp.zeros((NLOAD, 1), F32), slope)
    msg[...] = jnp.broadcast_to(rows[None], msg.shape)


def lengths(k, g, codes_rows, scal):
    sums = jnp.sum(g.reshape(128, 8, 128), axis=0)
    curve, cross = sums[6:7], sums[7:8]
    length = jnp.where(codes_rows[k : k + 1] == 1, -1.0, scal[0:1] / curve)
    return length, curve, cross


def update_kernel(
    k, g, vh, vl, codes, codes_rows, scal, point, gradient, q, image, act, par, t_stack, bh, bl,
    point_out, gradient_out, u, scal_out, msg,
):
    got = g[...]
    length, curve, cross = lengths(k, got, codes_rows, scal)
    scal_out[0:1, :] = length
    scal_out[1:2, :] = curve
    scal_out[2:3, :] = cross
    scal_out[3:8, :] = jnp.zeros((5, 128), F32)
    step = flip(jnp.broadcast_to(length, (8, 128)))[:NLOAD, 0:1]
    factor = spread(coarse(vh[...], vl[...], got))
    code = codes[:, k + 1 : k + 2]
    coef_t = jnp.zeros((NLOAD, 128), F32)
    slope = jnp.zeros((NLOAD, 1), F32)
    bend = jnp.zeros((NLOAD, 1), F32)
    for at, width in SEGS:
        seg = slice(at, at + width)
        w = image[:, seg] - mm(factor, t_stack[:, seg])
        m = point[:, seg] - step * q[:, seg]
        grad = gradient[:, seg] - step * w
        point_out[:, seg] = m
        gradient_out[:, seg] = grad
        x, slope_part, bend_part = next_part(seg, at, code, m, grad, w, act[...], weight(par, at))
        u[:, seg] = x
        slope += slope_part
        bend += bend_part
        coef_t += project_rows(x, bh[seg, :], bl[seg, :])
    msg[...] = jnp.broadcast_to(message(coef_t, bend, slope)[None], msg.shape)


def last_update_kernel(
    k, g, vh, vl, codes_rows, scal, point, gradient, q, image, t_stack, o_s, o_g, o_c,
    point_out, gradient_out,
):
    got = g[...]
    length, _, _ = lengths(k, got, codes_rows, scal)
    step = flip(jnp.broadcast_to(length, (8, 128)))[:NLOAD, 0:1]
    factor = spread(coarse(vh[...], vl[...], got))
    for at, width in SEGS:
        seg = slice(at, at + width)
        w = image[:, seg] - mm(factor, t_stack[:, seg])
        m = point[:, seg] - step * q[:, seg]
        grad = gradient[:, seg] - step * w
        order = {512: o_s, 1536: o_g, 2048: o_c}.get(at)
        if order is not None:
            m = shuffle_back(m, order[...])
            grad = shuffle_back(grad, order[...])
        point_out[:, seg] = m
        gradient_out[:, seg] = grad


VMEM_BYTES = 24 * 2**20


def call(kernel, outs, *operands, flops=0):
    moved = sum(x.size * x.dtype.itemsize for x in operands) + sum(
        o.size * o.dtype.itemsize for o in outs
    )
    return pl.pallas_call(
        kernel,
        out_shape=outs,
        compiler_params=pltpu.CompilerParams(vmem_limit_bytes=VMEM_BYTES),
        cost_estimate=pl.CostEstimate(flops=flops, bytes_accessed=moved, transcendentals=0),
    )(*operands)


def whole(shape):
    return pl.BlockSpec(shape, lambda i: (0,) * len(shape))


def columns_of(rows):
    return pl.BlockSpec((rows, FACE), lambda i: (0, i))


def call_columns(kernel, outs, fixed, streamed):
    return pl.pallas_call(
        kernel,
        grid=(ORDER // FACE,),
        in_specs=[whole(x.shape) for x in fixed] + [columns_of(x.shape[0]) for x in streamed],
        out_specs=[whole(o.shape) for o in outs],
        out_shape=outs,
        scratch_shapes=[pltpu.VMEM((NLOAD, ORDER), BF16)],
        compiler_params=pltpu.CompilerParams(vmem_limit_bytes=VMEM_BYTES),
        cost_estimate=pl.CostEstimate(
            flops=2 * NLOAD * ORDER * ORDER, bytes_accessed=30 * 2**20, transcendentals=0
        ),
    )(*fixed, *streamed)


def shards(
    schur,
    coarse_basis,
    coarse_inverse,
    coarse_coeff,
    dual_load,
    face_order,
    contact_partner,
    active_flags,
    step_codes,
):
    subs, groups = lax.axis_size("sub"), lax.axis_size("grp")
    count = subs * groups
    quarter = groups // 4
    i, j = lax.axis_index("sub"), lax.axis_index("grp")
    sub_pairs = [(s, s + 1) for s in range(subs - 1)]
    grp_pairs = [(s, s + 1) for s in range(groups - 1) if s + 1 not in (quarter, 3 * quarter)]
    across = [(s, (s + groups // 2) % groups) for s in range(groups)]

    def swaps(pairs, odd):
        chosen = [(a, b) for a, b in pairs if a % 2 == odd]
        return chosen + [(b, a) for a, b in chosen]

    def exchange(xa, xb, ya, yb, xc):
        rc = lax.ppermute(xc, "grp", across)
        ra = lax.ppermute(xa, "sub", swaps(sub_pairs, 0))
        rb = lax.ppermute(xb, "sub", swaps(sub_pairs, 1))
        sb = lax.ppermute(yb, "grp", swaps(grp_pairs, 1))
        sa = lax.ppermute(ya, "grp", swaps(grp_pairs, 0))
        return ra, rb, sa, sb, rc

    def gathered(rows):
        return lax.all_to_all(rows, AXES, 0, 0).reshape(count * 8, 128)

    def half(flag):
        return jnp.where(flag, 0.5, 1.0).astype(F32)

    def wide(value, width=FACE):
        return jnp.full((1, width), value, F32)

    schur_block = schur[0]
    lower_g = (j > 0) & (j != quarter) & (j != 3 * quarter)
    upper_g = (j < groups - 1) & (j != quarter - 1) & (j != 3 * quarter - 1)
    par = jnp.concatenate(
        [
            wide((i % 2 == 0).astype(F32)),
            wide((j % 2 == 0).astype(F32)),
            wide(half(i > 0)),
            wide(half(i < subs - 1)),
            wide(half(lower_g)),
            wide(half(upper_g)),
            jnp.zeros((2, FACE), F32),
        ]
    )
    blocks = coarse_inverse.reshape(MODES, count, MODES)
    vp = jnp.pad(blocks, ((0, 2), (0, 0), (0, 2))).reshape(8, count * 8)
    columns = jnp.pad(blocks.transpose(1, 0, 2), ((0, 0), (0, 2), (NLOAD, 128 - NLOAD - MODES)))
    partner = jnp.where(j >= groups // 2, contact_partner, jnp.arange(CONT, dtype=jnp.int32)[None])

    field = sds((NLOAD, ORDER))
    small = sds((8, 128))
    ready = sds((count, 8, 128))
    buffers = [sds((NLOAD, FACE))] * 4 + [sds((NLOAD, CONT))]

    o_s, o_g, o_c, basis, coeff, act, code_columns, code_rows, *faces = call(
        prepare_kernel,
        [sds((FACE, FACE), BF16)] * 2
        + [sds((CONT, CONT), BF16), sds((8, ORDER)), small, sds((NLOAD, CONT))]
        + [sds((NLOAD, 128)), small]
        + [sds((32, FACE))] * 4
        + [sds((48, CONT))],
        coarse_basis[0], vp, coarse_coeff[0], face_order[0], partner, active_flags[0], step_codes, par,
    )
    t_stack, vh, vl, bh, bl, point, msg = call(
        start_kernel,
        [sds((256, ORDER), BF16)]
        + [sds((48, count * 8), BF16)] * 2
        + [sds((ORDER, 128), BF16)] * 2
        + [field, ready],
        basis, vp, coeff, par, columns, *exchange(*faces),
    )
    orders = (o_s, o_g, o_c)

    got = gathered(msg)
    gh, gl, z, *faces = call_columns(
        first_search_kernel,
        [sds((16, count * 8), BF16)] * 2 + [field] + buffers,
        (got, vh, vl, par, point, t_stack) + orders,
        (dual_load[0], schur_block),
    )
    image, msg = call(first_image_kernel, [field, ready], z, *exchange(*faces), par, bh, bl)
    got = gathered(msg)
    gradient, u, msg = call(
        first_update_kernel,
        [field, field, ready],
        got, vh, vl, code_columns, point, image, act, par, t_stack, bh, bl,
    )
    q = u
    scal = jnp.zeros((8, 128), F32)
    coef_q = jnp.zeros((56, 128), F32)
    for k in range(ITERS):
        got = gathered(msg)
        coef_u, coef_q, scal, q, z, *faces = call_columns(
            functools.partial(search_kernel, k),
            [sds((56, 128))] * 2 + [small, field, field] + buffers,
            (got, vh, vl, gh, gl, code_rows, scal, coef_q, par, u, q, t_stack) + orders,
            (schur_block,),
        )
        image, msg = call(
            image_kernel,
            [field, ready],
            z, *exchange(*faces), par, q, u, coef_u, coef_q, bh, bl,
        )
        got = gathered(msg)
        if k < ITERS - 1:
            point, gradient, u, scal, msg = call(
                functools.partial(update_kernel, k),
                [field, field, field, small, ready],
                got, vh, vl, code_columns, code_rows, scal, point, gradient, q, image, act, par,
                t_stack, bh, bl,
            )
        else:
            point, gradient = call(
                functools.partial(last_update_kernel, k),
                [field, field],
                got, vh, vl, code_rows, scal, point, gradient, q, image, t_stack, *orders,
            )
    return (point[None], gradient[None])


def solution(mesh):
    in_specs = (
        P(AXES, None, None),
        P(AXES, None, None),
        P(AXES, None),
        P(AXES, None, None),
        P(AXES, None, None),
        P(AXES, None, None),
        P(AXES, None),
        P(AXES, None, None),
        P(),
    )
    out_specs = (P(AXES, None, None), P(AXES, None, None))
    return jax.shard_map(shards, mesh=mesh, in_specs=in_specs, out_specs=out_specs, check_vma=False)
```

time: 332 us -> 274 us (0.83)
  blocking collectives: 126 us -> 171 us
  starting transfers between devices: 67.3 us -> 24.2 us
  waiting for transfers between devices: 48.3 us -> 22.9 us
  Pallas kernels: 64.6 us -> 42.2 us
  local copies, waits for them, and re-layouts: 22.5 us -> 11.7 us
    all_to_all x6 -> x8, blocking collectives: 126 us -> 171 us  [gathered(): return lax.all_to_all(rows, AXES, 0, 0).reshape(count * 8, 128)]
    ppermute x25, starting transfers between devices: 55.7 us -> 24.2 us  [the longest x5 7.14 us: exchange(): sa = lax.ppermute(ya, 'grp', swaps(grp_pairs, 0))]
    all_to_all x2 -> x0, waiting for transfers between devices: 27.2 us -> none  [gathered(): return lax.all_to_all(rows, AXES, 0, 0).reshape(count * 8, 128)]
    pallas_call x8 -> x4, Pallas kernels: 38.9 us -> 25.9 us  [call_columns(): pl.pallas_call(kernel, grid=(ORDER // FACE,), in_specs=[whole(x.shape) fo...]
    all_to_all x2 -> x0, starting transfers between devices: 11.6 us -> none  [gathered(): return lax.all_to_all(rows, AXES, 0, 0).reshape(count * 8, 128)]
    pallas_call x11 -> x10, Pallas kernels: 25.7 us -> 16.3 us  [call(): pl.pallas_call(kernel, out_shape=outs, compiler_params=pltpu.CompilerPara...]
    unnamed x74 -> x19, local copies, waits for them, and re-layouts: 17 us -> 9.82 us
  transfers between devices with their start and end apart: 27 -> 25, of which waited for: 7 -> 5; matrix products, arithmetic and copies ran while one was open for 0% -> 0% of each run, Pallas kernels for 0% -> 0%
where the time goes in v2:
time: 274 us; the launch traced here: 273 us
  blocking collectives  171 us (62%)
  Pallas kernels  42.2 us (15%)
  starting transfers between devices  24.2 us (9%)
  waiting for transfers between devices  22.9 us (8%)
  local copies, waits for them, and re-layouts  11.7 us (4%)
    all_to_all x8, blocking collectives, gathered(): return lax.all_to_all(rows, AXES, 0, 0).reshape(count * 8, 128)  171 us
    pallas_call x4, Pallas kernels, call_columns(): pl.pallas_call(kernel, grid=(ORDER // FACE,), in_specs=[whole(x.shape) fo...  25.9 us
    ppermute x5, waiting for transfers between devices, exchange(): rc = lax.ppermute(xc, 'grp', across)  22.8 us
    pallas_call x10, Pallas kernels, call(): pl.pallas_call(kernel, out_shape=outs, compiler_params=pltpu.CompilerPara...  16.3 us
    unnamed x19, local copies, waits for them, and re-layouts  9.82 us
    ppermute x5, starting transfers between devices, exchange(): sa = lax.ppermute(ya, 'grp', swaps(grp_pairs, 0))  7.14 us
    ppermute x5, starting transfers between devices, exchange(): rc = lax.ppermute(xc, 'grp', across)  6.52 us
  transfers between devices with their start and end apart: 25, of which 5 were waited for; matrix products, arithmetic and copies ran while one was open for 0% of the time, Pallas kernels for 0%

profile of v2, /device:TPU:1, one launch (start us, length us, event | category | flops | bytes accessed | tf_op | source)
XLA Modules:
  0.0 273.3 jit_solution(5925893517522625869)
XLA Ops:
  0.7 0.7 copy.21
  1.4 0.8 copy.12.codes
  2.2 0.8 copy.20
  3.0 1.1 reshape.34
  4.6 0.9 copy-done.2
  5.4 0.7 copy-done.3
  6.1 1.1 shard_map.104
  7.3 2.1 collective-permute-start
  10.1 1.0 collective-permute-start.2
  11.7 4.3 %collective-permute-start.4 = (f32[48,256]{1,0:T(8,128)S(1)}, f32[48,256]{1,0:T(8,128)S(1)}, u32[]{:S(2)}, u32[]{:S(2)}) collective-permute-start(f32[48,256]{1,0:T(8,128)S(1)} %get-tuple-element.89), channel_id=1, source_target_pairs={{0,4},{1,5},{2,6},{3,7},{4,0},{5,1},{6,2},{7,3},{8,12},{9,13},{10,... | collective-permute-start | bytes 147464 | tf_op jit(solution)/shard_map/ppermute | solution.py:489
  16.5 1.0 collective-permute-done.4.rc
  17.6 1.8 shard_map.105
  19.4 27.2 %all_to_all.40 = f32[128,8,128]{2,1,0:T(8,128)S(1)} all-to-all(f32[128,8,128]{2,1,0:T(8,128)S(1)} %get-tuple-element.90), channel_id=1, replica_groups=mesh['sub'=16,'grp'=8] {'sub','grp'}, dimensions={0} | all-to-all | bytes 1048576 | tf_op jit(solution)/shard_map/all_to_all | solution.py:497
  46.6 4.7 %copy-done = bf16[1,2560,2560]{2,1,0:T(8,128)(2,1)S(1)} copy-done((bf16[1,2560,2560]{2,1,0:T(8,128)(2,1)S(1)}, bf16[1,2560,2560]{2,1,0:T(8,128)(2,1)}, u32[]{:S(2)}) %copy-start) | copy-done | bytes 13107224
  51.3 1.2 copy-done.1
  52.5 6.5 %shard_map.106 = (bf16[16,1024]{1,0:T(8,128)(2,1)S(1)}, bf16[16,1024]{1,0:T(8,128)(2,1)S(1)}, f32[96,2560]{1,0:T(8,128)S(1)}, f32[96,512]{1,0:T(8,128)S(1)}, f32...) custom-call(f32[1024,128]{1,0:T(8,128)S(1)} %bitcast.36, ...), custom_call_target="tpu_custom_call" | custom-call | flops 1258291200 | bytes 31457280 | tf_op jit(solution)/shard_map/pallas_call | solution.py:451
  59.5 0.7 collective-permute-start.6
  60.2 1.5 collective-permute-start.7
  61.7 0.7 collective-permute-start.8
  62.9 5.4 %collective-permute-done.9.rc = f32[96,256]{1,0:T(8,128)S(1)} collective-permute-done((f32[96,256]{1,0:T(8,128)S(1)}, f32[96,256]{1,0:T(8,128)S(1)}, u32[]{:S(2)}, u32[]{:S(2)}) %collective-permute-start.9) | collective-permute-done | bytes 98336 | tf_op jit(solution)/shard_map/ppermute | solution.py:489
  69.0 22.5 %all_to_all.41 = f32[128,8,128]{2,1,0:T(8,128)S(1)} all-to-all(f32[128,8,128]{2,1,0:T(8,128)S(1)} %get-tuple-element.106), channel_id=1, replica_groups=mesh['sub'=16,'grp'=8] {'sub','grp'}, dimensions={0} | all-to-all | bytes 1048576 | tf_op jit(solution)/shard_map/all_to_all | solution.py:497
  91.6 2.0 shard_map.108
  93.6 17.9 %all_to_all.42 = f32[128,8,128]{2,1,0:T(8,128)S(1)} all-to-all(f32[128,8,128]{2,1,0:T(8,128)S(1)} %get-tuple-element.110), channel_id=1, replica_groups=mesh['sub'=16,'grp'=8] {'sub','grp'}, dimensions={0} | all-to-all | bytes 1048576 | tf_op jit(solution)/shard_map/all_to_all | solution.py:497
  111.6 6.4 %shard_map.109 = (f32[56,128]{1,0:T(8,128)S(1)}, f32[56,128]{1,0:T(8,128)S(1)}, f32[8,128]{1,0:T(8,128)S(1)}, f32[96,2560]{1,0:T(8,128)S(1)}, f32[96,2560]{1,0:T...) custom-call(f32[1024,128]{1,0:T(8,128)S(1)} %bitcast.29, ...), custom_call_target="tpu_custom_call" | custom-call | flops 1258291200 | bytes 31457280 | tf_op jit(solution)/shard_map/pallas_call | solution.py:451
  118.5 0.7 collective-permute-start.11
  119.2 1.5 collective-permute-start.12
  120.7 0.7 collective-permute-start.13
  121.9 5.4 %collective-permute-done.14.rc = f32[96,256]{1,0:T(8,128)S(1)} collective-permute-done((f32[96,256]{1,0:T(8,128)S(1)}, f32[96,256]{1,0:T(8,128)S(1)}, u32[]{:S(2)}, u32[]{:S(2)}) %collective-permute-start.14) | collective-permute-done | bytes 98336 | tf_op jit(solution)/shard_map/ppermute | solution.py:489
  127.4 1.0 shard_map.110
  128.4 22.5 %all_to_all.43 = f32[128,8,128]{2,1,0:T(8,128)S(1)} all-to-all(f32[128,8,128]{2,1,0:T(8,128)S(1)} %get-tuple-element.124), channel_id=1, replica_groups=mesh['sub'=16,'grp'=8] {'sub','grp'}, dimensions={0} | all-to-all | bytes 1048576 | tf_op jit(solution)/shard_map/all_to_all | solution.py:497
  150.9 2.3 shard_map.111
  153.3 17.9 %all_to_all.44 = f32[128,8,128]{2,1,0:T(8,128)S(1)} all-to-all(f32[128,8,128]{2,1,0:T(8,128)S(1)} %get-tuple-element.128), channel_id=1, replica_groups=mesh['sub'=16,'grp'=8] {'sub','grp'}, dimensions={0} | all-to-all | bytes 1048576 | tf_op jit(solution)/shard_map/all_to_all | solution.py:497
  171.2 6.5 %shard_map.112 = (f32[56,128]{1,0:T(8,128)S(1)}, f32[56,128]{1,0:T(8,128)S(1)}, f32[8,128]{1,0:T(8,128)S(1)}, f32[96,2560]{1,0:T(8,128)S(1)}, f32[96,2560]{1,0:T...) custom-call(f32[1024,128]{1,0:T(8,128)S(1)} %bitcast.32, ...), custom_call_target="tpu_custom_call" | custom-call | flops 1258291200 | bytes 31457280 | tf_op jit(solution)/shard_map/pallas_call | solution.py:451
  178.8 1.5 collective-permute-start.17
  180.4 0.7 collective-permute-start.18
  181.6 5.4 %collective-permute-done.19.rc = f32[96,256]{1,0:T(8,128)S(1)} collective-permute-done((f32[96,256]{1,0:T(8,128)S(1)}, f32[96,256]{1,0:T(8,128)S(1)}, u32[]{:S(2)}, u32[]{:S(2)}) %collective-permute-start.19) | collective-permute-done | bytes 98336 | tf_op jit(solution)/shard_map/ppermute | solution.py:489
  187.1 0.9 shard_map.113
  188.0 22.5 %all_to_all.45 = f32[128,8,128]{2,1,0:T(8,128)S(1)} all-to-all(f32[128,8,128]{2,1,0:T(8,128)S(1)} %get-tuple-element.140), channel_id=1, replica_groups=mesh['sub'=16,'grp'=8] {'sub','grp'}, dimensions={0} | all-to-all | bytes 1048576 | tf_op jit(solution)/shard_map/all_to_all | solution.py:497
  210.5 2.4 shard_map.114
  212.9 17.9 %all_to_all.46 = f32[128,8,128]{2,1,0:T(8,128)S(1)} all-to-all(f32[128,8,128]{2,1,0:T(8,128)S(1)} %get-tuple-element.145), channel_id=1, replica_groups=mesh['sub'=16,'grp'=8] {'sub','grp'}, dimensions={0} | all-to-all | bytes 1048576 | tf_op jit(solution)/shard_map/all_to_all | solution.py:497
  230.8 6.5 %shard_map.115 = (f32[56,128]{1,0:T(8,128)S(1)}, f32[56,128]{1,0:T(8,128)S(1)}, f32[8,128]{1,0:T(8,128)S(1)}, f32[96,2560]{1,0:T(8,128)S(1)}, f32[96,2560]{1,0:T...) custom-call(f32[1024,128]{1,0:T(8,128)S(1)} %bitcast.30, ...), custom_call_target="tpu_custom_call" | custom-call | flops 1258291200 | bytes 31457280 | tf_op jit(solution)/shard_map/pallas_call | solution.py:451
  237.8 0.7 collective-permute-start.21
  238.5 1.5 collective-permute-start.22
  240.0 0.7 collective-permute-start.23
  241.2 5.4 %collective-permute-done.24.rc = f32[96,256]{1,0:T(8,128)S(1)} collective-permute-done((f32[96,256]{1,0:T(8,128)S(1)}, f32[96,256]{1,0:T(8,128)S(1)}, u32[]{:S(2)}, u32[]{:S(2)}) %collective-permute-start.24) | collective-permute-done | bytes 98336 | tf_op jit(solution)/shard_map/ppermute | solution.py:489
  246.7 0.9 shard_map.116
  247.6 22.5 %all_to_all.47 = f32[128,8,128]{2,1,0:T(8,128)S(1)} all-to-all(f32[128,8,128]{2,1,0:T(8,128)S(1)} %get-tuple-element.157), channel_id=1, replica_groups=mesh['sub'=16,'grp'=8] {'sub','grp'}, dimensions={0} | all-to-all | bytes 1048576 | tf_op jit(solution)/shard_map/all_to_all | solution.py:497
  270.1 3.2 %shard_map.117 = (f32[96,2560]{1,0:T(8,128)}, f32[96,2560]{1,0:T(8,128)}) custom-call(f32[1024,128]{1,0:T(8,128)S(1)} %bitcast.34, bf16[48,1024]{1,0:T(8,128)(2,1)S(1)} %get-tuple-element.91.vh, bf16[48,1024]{1,0:T(8,128)(2,1)S(1)} %get-tuple-element.92.vl, f32[8,128]{1,0:T(8,128)S(1)} %get-tuple-element.113.codes.codes_rows, ...), custom_call_target="tpu_custom_call" | custom-call | bytes 9117696 | tf_op jit(solution)/shard_map/pallas_call | solution.py:434
  (60 shorter events, 7.6 us)
Async XLA Ops:
  4.5 0.9 copy-start.2
  5.4 0.7 copy-start.3
  7.3 10.3 %collective-permute-start = (f32[32,512]{1,0:T(8,128)S(1)}, f32[32,512]{1,0:T(8,128)S(1)}, u32[]{:S(2)}, u32[]{:S(2)}) collective-permute-start(f32[32,512]{1,0:T(8,128)S(1)} %get-tuple-element.85), channel_id=1, source_target_pairs={{0,8},{16,24},{32,40},{48,56},{64,72},{80,88},{96,104},{112,120},{... | collective-permute-start | bytes 196616 | tf_op jit(solution)/shard_map/ppermute | solution.py:490
  9.4 8.2 %collective-permute-start.1 = (f32[32,512]{1,0:T(8,128)S(1)}, f32[32,512]{1,0:T(8,128)S(1)}, u32[]{:S(2)}, u32[]{:S(2)}) collective-permute-start(f32[32,512]{1,0:T(8,128)S(1)} %get-tuple-element.86), channel_id=1, source_target_pairs={{8,16},{24,32},{40,48},{56,64},{72,80},{88,96},{104,112},{16,8},{3... | collective-permute-start | bytes 196616 | tf_op jit(solution)/shard_map/ppermute | solution.py:491
  10.1 7.5 %collective-permute-start.2 = (f32[32,512]{1,0:T(8,128)S(1)}, f32[32,512]{1,0:T(8,128)S(1)}, u32[]{:S(2)}, u32[]{:S(2)}) collective-permute-start(f32[32,512]{1,0:T(8,128)S(1)} %get-tuple-element.87), channel_id=1, source_target_pairs={{0,1},{2,3},{4,5},{6,7},{1,0},{3,2},{5,4},{7,6},{8,9},{10,11},{12,... | collective-permute-start | bytes 196616 | tf_op jit(solution)/shard_map/ppermute | solution.py:493
  11.1 6.5 %collective-permute-start.3 = (f32[32,512]{1,0:T(8,128)S(1)}, f32[32,512]{1,0:T(8,128)S(1)}, u32[]{:S(2)}, u32[]{:S(2)}) collective-permute-start(f32[32,512]{1,0:T(8,128)S(1)} %get-tuple-element.88), channel_id=1, source_target_pairs={{3,4},{4,3},{11,12},{12,11},{19,20},{20,19},{27,28},{28,27},{35,36... | collective-permute-start | bytes 196616 | tf_op jit(solution)/shard_map/ppermute | solution.py:492
  11.7 5.8 %collective-permute-start.4 = (f32[48,256]{1,0:T(8,128)S(1)}, f32[48,256]{1,0:T(8,128)S(1)}, u32[]{:S(2)}, u32[]{:S(2)}) collective-permute-start(f32[48,256]{1,0:T(8,128)S(1)} %get-tuple-element.89), channel_id=1, source_target_pairs={{0,4},{1,5},{2,6},{3,7},{4,0},{5,1},{6,2},{7,3},{8,12},{9,13},{10,... | collective-permute-start | bytes 147464 | tf_op jit(solution)/shard_map/ppermute | solution.py:489
  46.6 4.7 %copy-start = (bf16[1,2560,2560]{2,1,0:T(8,128)(2,1)S(1)}, bf16[1,2560,2560]{2,1,0:T(8,128)(2,1)}, u32[]{:S(2)}) copy-start(bf16[1,2560,2560]{2,1,0:T(8,128)(2,1)} %param.9) | copy-start | bytes 39321604
  51.3 1.2 copy-start.1
  52.5 59.1 %slice-start = ((s8[13107200]{0:T(1024)(128)(4,1)}), s8[4194304]{0:T(1024)(128)(4,1)S(1)}, s32[]{:S(2)}) async-start(s8[13107200]{0:T(1024)(128)(4,1)} %bitcast.24), calls=%async_computation.8 | async-start | bytes 8388608
  52.5 59.1 %slice-start.1 = ((s8[13107200]{0:T(1024)(128)(4,1)}), s8[4194304]{0:T(1024)(128)(4,1)S(1)}, s32[]{:S(2)}) async-start(s8[13107200]{0:T(1024)(128)(4,1)} %bitcast.24), calls=%async_computation.9 | async-start | bytes 8388608
  52.5 59.1 %slice-start.2 = ((s8[13107200]{0:T(1024)(128)(4,1)}), s8[4194304]{0:T(1024)(128)(4,1)S(1)}, s32[]{:S(2)}) async-start(s8[13107200]{0:T(1024)(128)(4,1)} %bitcast.24), calls=%async_computation.10 | async-start | bytes 8388608
  59.0 9.3 %collective-permute-start.5 = (f32[96,512]{1,0:T(8,128)S(1)}, f32[96,512]{1,0:T(8,128)S(1)}, u32[]{:S(2)}, u32[]{:S(2)}) collective-permute-start(f32[96,512]{1,0:T(8,128)S(1)} %get-tuple-element.99), channel_id=1, source_target_pairs={{0,8},{16,24},{32,40},{48,56},{64,72},{80,88},{96,104},{112,120},{... | collective-permute-start | bytes 589832 | tf_op jit(solution)/shard_map/ppermute | solution.py:490
  59.5 8.9 %collective-permute-start.6 = (f32[96,512]{1,0:T(8,128)S(1)}, f32[96,512]{1,0:T(8,128)S(1)}, u32[]{:S(2)}, u32[]{:S(2)}) collective-permute-start(f32[96,512]{1,0:T(8,128)S(1)} %get-tuple-element.100), channel_id=1, source_target_pairs={{8,16},{24,32},{40,48},{56,64},{72,80},{88,96},{104,112},{16,8},{3... | collective-permute-start | bytes 589832 | tf_op jit(solution)/shard_map/ppermute | solution.py:491
  60.2 8.2 %collective-permute-start.7 = (f32[96,512]{1,0:T(8,128)S(1)}, f32[96,512]{1,0:T(8,128)S(1)}, u32[]{:S(2)}, u32[]{:S(2)}) collective-permute-start(f32[96,512]{1,0:T(8,128)S(1)} %get-tuple-element.101), channel_id=1, source_target_pairs={{0,1},{2,3},{4,5},{6,7},{1,0},{3,2},{5,4},{7,6},{8,9},{10,11},{12,... | collective-permute-start | bytes 589832 | tf_op jit(solution)/shard_map/ppermute | solution.py:493
  61.7 6.7 %collective-permute-start.8 = (f32[96,512]{1,0:T(8,128)S(1)}, f32[96,512]{1,0:T(8,128)S(1)}, u32[]{:S(2)}, u32[]{:S(2)}) collective-permute-start(f32[96,512]{1,0:T(8,128)S(1)} %get-tuple-element.102), channel_id=1, source_target_pairs={{3,4},{4,3},{11,12},{12,11},{19,20},{20,19},{27,28},{28,27},{35,36... | collective-permute-start | bytes 589832 | tf_op jit(solution)/shard_map/ppermute | solution.py:492
  62.3 6.0 %collective-permute-start.9 = (f32[96,256]{1,0:T(8,128)S(1)}, f32[96,256]{1,0:T(8,128)S(1)}, u32[]{:S(2)}, u32[]{:S(2)}) collective-permute-start(f32[96,256]{1,0:T(8,128)S(1)} %get-tuple-element.103), channel_id=1, source_target_pairs={{0,4},{1,5},{2,6},{3,7},{4,0},{5,1},{6,2},{7,3},{8,12},{9,13},{10,... | collective-permute-start | bytes 294920 | tf_op jit(solution)/shard_map/ppermute | solution.py:489
  69.0 42.6 %slice-start.3 = ((s8[13107200]{0:T(1024)(128)(4,1)}), s8[524288]{0:T(1024)(128)(4,1)S(1)}, s32[]{:S(2)}) async-start(s8[13107200]{0:T(1024)(128)(4,1)} %bitcast.24), calls=%async_computation.11 | async-start | bytes 1048576
  118.1 9.3 %collective-permute-start.10 = (f32[96,512]{1,0:T(8,128)S(1)}, f32[96,512]{1,0:T(8,128)S(1)}, u32[]{:S(2)}, u32[]{:S(2)}) collective-permute-start(f32[96,512]{1,0:T(8,128)S(1)} %get-tuple-element.116), channel_id=1, source_target_pairs={{0,8},{16,24},{32,40},{48,56},{64,72},{80,88},{96,104},{112,120},{... | collective-permute-start | bytes 589832 | tf_op jit(solution)/shard_map/ppermute | solution.py:490
  118.5 8.9 %collective-permute-start.11 = (f32[96,512]{1,0:T(8,128)S(1)}, f32[96,512]{1,0:T(8,128)S(1)}, u32[]{:S(2)}, u32[]{:S(2)}) collective-permute-start(f32[96,512]{1,0:T(8,128)S(1)} %get-tuple-element.117), channel_id=1, source_target_pairs={{8,16},{24,32},{40,48},{56,64},{72,80},{88,96},{104,112},{16,8},{3... | collective-permute-start | bytes 589832 | tf_op jit(solution)/shard_map/ppermute | solution.py:491
  119.2 8.2 %collective-permute-start.12 = (f32[96,512]{1,0:T(8,128)S(1)}, f32[96,512]{1,0:T(8,128)S(1)}, u32[]{:S(2)}, u32[]{:S(2)}) collective-permute-start(f32[96,512]{1,0:T(8,128)S(1)} %get-tuple-element.118), channel_id=1, source_target_pairs={{0,1},{2,3},{4,5},{6,7},{1,0},{3,2},{5,4},{7,6},{8,9},{10,11},{12,... | collective-permute-start | bytes 589832 | tf_op jit(solution)/shard_map/ppermute | solution.py:493
  120.7 6.7 %collective-permute-start.13 = (f32[96,512]{1,0:T(8,128)S(1)}, f32[96,512]{1,0:T(8,128)S(1)}, u32[]{:S(2)}, u32[]{:S(2)}) collective-permute-start(f32[96,512]{1,0:T(8,128)S(1)} %get-tuple-element.119), channel_id=1, source_target_pairs={{3,4},{4,3},{11,12},{12,11},{19,20},{20,19},{27,28},{28,27},{35,36... | collective-permute-start | bytes 589832 | tf_op jit(solution)/shard_map/ppermute | solution.py:492
  121.4 6.0 %collective-permute-start.14 = (f32[96,256]{1,0:T(8,128)S(1)}, f32[96,256]{1,0:T(8,128)S(1)}, u32[]{:S(2)}, u32[]{:S(2)}) collective-permute-start(f32[96,256]{1,0:T(8,128)S(1)} %get-tuple-element.120), channel_id=1, source_target_pairs={{0,4},{1,5},{2,6},{3,7},{4,0},{5,1},{6,2},{7,3},{8,12},{9,13},{10,... | collective-permute-start | bytes 294920 | tf_op jit(solution)/shard_map/ppermute | solution.py:489
  177.7 9.3 %collective-permute-start.15 = (f32[96,512]{1,0:T(8,128)S(1)}, f32[96,512]{1,0:T(8,128)S(1)}, u32[]{:S(2)}, u32[]{:S(2)}) collective-permute-start(f32[96,512]{1,0:T(8,128)S(1)} %get-tuple-element.132), channel_id=1, source_target_pairs={{0,8},{16,24},{32,40},{48,56},{64,72},{80,88},{96,104},{112,120},{... | collective-permute-start | bytes 589832 | tf_op jit(solution)/shard_map/ppermute | solution.py:490
  178.2 8.9 %collective-permute-start.16 = (f32[96,512]{1,0:T(8,128)S(1)}, f32[96,512]{1,0:T(8,128)S(1)}, u32[]{:S(2)}, u32[]{:S(2)}) collective-permute-start(f32[96,512]{1,0:T(8,128)S(1)} %get-tuple-element.133), channel_id=1, source_target_pairs={{8,16},{24,32},{40,48},{56,64},{72,80},{88,96},{104,112},{16,8},{3... | collective-permute-start | bytes 589832 | tf_op jit(solution)/shard_map/ppermute | solution.py:491
  178.8 8.2 %collective-permute-start.17 = (f32[96,512]{1,0:T(8,128)S(1)}, f32[96,512]{1,0:T(8,128)S(1)}, u32[]{:S(2)}, u32[]{:S(2)}) collective-permute-start(f32[96,512]{1,0:T(8,128)S(1)} %get-tuple-element.134), channel_id=1, source_target_pairs={{0,1},{2,3},{4,5},{6,7},{1,0},{3,2},{5,4},{7,6},{8,9},{10,11},{12,... | collective-permute-start | bytes 589832 | tf_op jit(solution)/shard_map/ppermute | solution.py:493
  180.4 6.7 %collective-permute-start.18 = (f32[96,512]{1,0:T(8,128)S(1)}, f32[96,512]{1,0:T(8,128)S(1)}, u32[]{:S(2)}, u32[]{:S(2)}) collective-permute-start(f32[96,512]{1,0:T(8,128)S(1)} %get-tuple-element.135), channel_id=1, source_target_pairs={{3,4},{4,3},{11,12},{12,11},{19,20},{20,19},{27,28},{28,27},{35,36... | collective-permute-start | bytes 589832 | tf_op jit(solution)/shard_map/ppermute | solution.py:492
  181.0 6.0 %collective-permute-start.19 = (f32[96,256]{1,0:T(8,128)S(1)}, f32[96,256]{1,0:T(8,128)S(1)}, u32[]{:S(2)}, u32[]{:S(2)}) collective-permute-start(f32[96,256]{1,0:T(8,128)S(1)} %get-tuple-element.136), channel_id=1, source_target_pairs={{0,4},{1,5},{2,6},{3,7},{4,0},{5,1},{6,2},{7,3},{8,12},{9,13},{10,... | collective-permute-start | bytes 294920 | tf_op jit(solution)/shard_map/ppermute | solution.py:489
  237.3 9.3 %collective-permute-start.20 = (f32[96,512]{1,0:T(8,128)S(1)}, f32[96,512]{1,0:T(8,128)S(1)}, u32[]{:S(2)}, u32[]{:S(2)}) collective-permute-start(f32[96,512]{1,0:T(8,128)S(1)} %get-tuple-element.149), channel_id=1, source_target_pairs={{0,8},{16,24},{32,40},{48,56},{64,72},{80,88},{96,104},{112,120},{... | collective-permute-start | bytes 589832 | tf_op jit(solution)/shard_map/ppermute | solution.py:490
  237.8 8.9 %collective-permute-start.21 = (f32[96,512]{1,0:T(8,128)S(1)}, f32[96,512]{1,0:T(8,128)S(1)}, u32[]{:S(2)}, u32[]{:S(2)}) collective-permute-start(f32[96,512]{1,0:T(8,128)S(1)} %get-tuple-element.150), channel_id=1, source_target_pairs={{8,16},{24,32},{40,48},{56,64},{72,80},{88,96},{104,112},{16,8},{3... | collective-permute-start | bytes 589832 | tf_op jit(solution)/shard_map/ppermute | solution.py:491
  238.5 8.2 %collective-permute-start.22 = (f32[96,512]{1,0:T(8,128)S(1)}, f32[96,512]{1,0:T(8,128)S(1)}, u32[]{:S(2)}, u32[]{:S(2)}) collective-permute-start(f32[96,512]{1,0:T(8,128)S(1)} %get-tuple-element.151), channel_id=1, source_target_pairs={{0,1},{2,3},{4,5},{6,7},{1,0},{3,2},{5,4},{7,6},{8,9},{10,11},{12,... | collective-permute-start | bytes 589832 | tf_op jit(solution)/shard_map/ppermute | solution.py:493
  240.0 6.7 %collective-permute-start.23 = (f32[96,512]{1,0:T(8,128)S(1)}, f32[96,512]{1,0:T(8,128)S(1)}, u32[]{:S(2)}, u32[]{:S(2)}) collective-permute-start(f32[96,512]{1,0:T(8,128)S(1)} %get-tuple-element.152), channel_id=1, source_target_pairs={{3,4},{4,3},{11,12},{12,11},{19,20},{20,19},{27,28},{28,27},{35,36... | collective-permute-start | bytes 589832 | tf_op jit(solution)/shard_map/ppermute | solution.py:492
  240.7 6.0 %collective-permute-start.24 = (f32[96,256]{1,0:T(8,128)S(1)}, f32[96,256]{1,0:T(8,128)S(1)}, u32[]{:S(2)}, u32[]{:S(2)}) collective-permute-start(f32[96,256]{1,0:T(8,128)S(1)} %get-tuple-element.153), channel_id=1, source_target_pairs={{0,4},{1,5},{2,6},{3,7},{4,0},{5,1},{6,2},{7,3},{8,12},{9,13},{10,... | collective-permute-start | bytes 294920 | tf_op jit(solution)/shard_map/ppermute | solution.py:489

commit v3 on v2

--- a/solution.py
+++ b/solution.py
@@ -128,7 +128,7 @@
 
 def prepare_kernel(
     basis, vp, coeff, face_rows, contact_row, flags, codes, par,
-    o_s, o_g, o_c, basis_out, coeff_out, act_out, code_columns, code_rows, xa, xb, ya, yb, mc,
+    o_s, o_g, o_c, basis_out, coeff_out, act_out, code_columns, code_rows, mc, xb, xa, yb, ya,
 ):
     for row, out in ((face_rows[0:1, :], o_s), (face_rows[1:2, :], o_g), (contact_row[...], o_c)):
         n = row.shape[1]
@@ -164,9 +164,10 @@
 
 
 def start_kernel(
-    basis, vp, coeff, par, columns, xa, xb, ya, yb, rc,
+    basis, vp, coeff, par, columns, early_schur, early_load, xa, xb, ya, yb, rc,
     t_stack, vh, vl, bh, bl, point, msg,
 ):
+    del early_schur, early_load
     zero8 = jnp.zeros((8, ORDER), F32)
     pieces = [basis[...]]
     rows = [vp[...]]
@@ -209,88 +210,73 @@
     return x if order is None else mm(x, order[...]).astype(BF16)
 
 
-def product_block(p, schur, orders, z, load=None):
-    step = pl.program_id(0)
-    y = mm(p[...], schur[...])
-    if load is not None:
-        y = y - load[...]
-    for n in range(5):
-
-        @pl.when(step == n)
-        def _():
-            x = y
-            if n == 4:
-                x = jnp.concatenate([shuffle(x[:, :CONT], orders[2][...]), x[:, CONT:]], axis=1)
-            elif n in (1, 3):
-                x = shuffle(x, orders[n // 2][...])
-            z[:, FACE * n : FACE * (n + 1)] = x
-
-
-def send_product(par, z, xa, xb, ya, yb, xc):
-    @pl.when(pl.program_id(0) == 4)
-    def _():
-        send_faces(par, [z[:, FACE * n : FACE * (n + 1)] for n in range(4)], (xa, xb, ya, yb))
-        xc[...] = z[:, CON : CON + CONT]
+def product(p, schur, orders, par, z, xc, xb, xa, yb, ya, load=None):
+    faces = {}
+    for n in (4, 0, 1, 2, 3):
+        seg = slice(FACE * n, FACE * (n + 1))
+        x = mm(p[...], schur[:, seg])
+        if load is not None:
+            x = x - load[:, seg]
+        if n == 4:
+            x = jnp.concatenate([shuffle(x[:, :CONT], orders[2][...]), x[:, CONT:]], axis=1)
+        elif n in (1, 3):
+            x = shuffle(x, orders[n // 2][...])
+        z[:, seg] = x
+    send_faces(par, [z[:, FACE * n : FACE * (n + 1)] for n in range(4)], (xa, xb, ya, yb))
+    xc[...] = z[:, CON : CON + CONT]
 
 
 def first_search_kernel(
     g, vh, vl, par, u, t_stack, o_s, o_g, o_c, load, schur,
-    gh, gl, z, xa, xb, ya, yb, xc, p,
+    gh, gl, z, xc, xb, xa, yb, ya, p,
 ):
     orders = (o_s, o_g, o_c)
 
-    @pl.when(pl.program_id(0) == 0)
-    def _():
-        column = flip(g[...])[96:112]
-        row = lax.broadcasted_iota(jnp.int32, column.shape, 0)
-        hi, low = split2(jnp.where(row < MODES, column, 0.0))
-        gh[...] = hi
-        gl[...] = low
-        factor = spread(coarse(vh[...], vl[...], g[...]))
-        for at, width in SEGS:
-            seg = slice(at, at + width)
-            p[:, seg] = rounded(u[:, seg] - mm(factor, t_stack[:, seg]), at, orders)
-
-    product_block(p, schur, orders, z, load)
-    send_product(par, z, xa, xb, ya, yb, xc)
+    column = flip(g[...])[96:112]
+    row = lax.broadcasted_iota(jnp.int32, column.shape, 0)
+    hi, low = split2(jnp.where(row < MODES, column, 0.0))
+    gh[...] = hi
+    gl[...] = low
+    factor = spread(coarse(vh[...], vl[...], g[...]))
+    for at, width in SEGS:
+        seg = slice(at, at + width)
+        p[:, seg] = rounded(u[:, seg] - mm(factor, t_stack[:, seg]), at, orders)
+    product(p, schur, orders, par, z, xc, xb, xa, yb, ya, load)
 
 
 def search_kernel(
     k, g, vh, vl, gh, gl, codes, scal, prev, par, u, d, t_stack, o_s, o_g, o_c, schur,
-    coef_u, coef_q, scal_out, q, z, xa, xb, ya, yb, xc, p,
+    coef_u, coef_q, scal_out, q, z, xc, xb, xa, yb, ya, p,
 ):
     orders = (o_s, o_g, o_c)
 
-    @pl.when(pl.program_id(0) == 0)
-    def _():
-        got = g[...]
-        gah, gal = split2(got)
-        alpha = mm(vh[...], gah) + mm(vl[...], gah) + mm(vh[...], gal)
-        gamma = (mm(gh[...], gah) + mm(gl[...], gah) + mm(gh[...], gal))[:8]
-        sums = jnp.sum(got.reshape(128, 8, 128), axis=0)
-        mix = jnp.concatenate([alpha, gamma], axis=0)
-        coef_u[...] = mix
-        scal_out[0:1, :] = sums[7:8]
-        scal_out[1:8, :] = jnp.zeros((7, 128), F32)
+    got = g[...]
+    gah, gal = split2(got)
+    alpha = mm(vh[...], gah) + mm(vl[...], gah) + mm(vh[...], gal)
+    gamma = (mm(gh[...], gah) + mm(gl[...], gah) + mm(gh[...], gal))[:8]
+    sums = jnp.sum(got.reshape(128, 8, 128), axis=0)
+    mix = jnp.concatenate([alpha, gamma], axis=0)
+    coef_u[...] = mix
+    scal_out[0:1, :] = sums[7:8]
+    scal_out[1:8, :] = jnp.zeros((7, 128), F32)
+    if k > 0:
+        bend = sums[6:7]
+        length, curve, cross = scal[0:1], scal[1:2], scal[2:3]
+        both = (codes[k : k + 1] == 0) & (codes[k - 1 : k] == 0)
+        factor2 = jnp.where(both, (cross - length * bend) / curve, 0.0)
+        mix = jnp.where(factor2 == 0.0, mix, mix - factor2 * prev[...])
+        g2 = flip(jnp.broadcast_to(factor2, (8, 128)))[:NLOAD, 0:1]
+    coef_q[...] = mix
+    factor = spread(mix[:48])
+    for at, width in SEGS:
+        seg = slice(at, at + width)
+        x = u[:, seg]
         if k > 0:
-            bend = sums[6:7]
-            length, curve, cross = scal[0:1], scal[1:2], scal[2:3]
-            both = (codes[k : k + 1] == 0) & (codes[k - 1 : k] == 0)
-            factor2 = jnp.where(both, (cross - length * bend) / curve, 0.0)
-            mix = jnp.where(factor2 == 0.0, mix, mix - factor2 * prev[...])
-            g2 = flip(jnp.broadcast_to(factor2, (8, 128)))[:NLOAD, 0:1]
-        coef_q[...] = mix
-        factor = spread(mix[:48])
-        for at, width in SEGS:
-            seg = slice(at, at + width)
-            x = u[:, seg]
-            if k > 0:
-                x = x - g2 * d[:, seg]
-            q[:, seg] = x
-            p[:, seg] = rounded(x - mm(factor, t_stack[:, seg]), at, orders)
-
-    product_block(p, schur, orders, z)
-    send_product(par, z, xa, xb, ya, yb, xc)
+            x = x - g2 * d[:, seg]
+        q[:, seg] = x
+        p[:, seg] = rounded(x - mm(factor, t_stack[:, seg]), at, orders)
+
+    product(p, schur, orders, par, z, xc, xb, xa, yb, ya)
 
 
 def image_kernel(
@@ -439,27 +425,16 @@
     )(*operands)
 
 
-def whole(shape):
-    return pl.BlockSpec(shape, lambda i: (0,) * len(shape))
-
-
-def columns_of(rows):
-    return pl.BlockSpec((rows, FACE), lambda i: (0, i))
-
-
-def call_columns(kernel, outs, fixed, streamed):
+def call_product(kernel, outs, *operands):
     return pl.pallas_call(
         kernel,
-        grid=(ORDER // FACE,),
-        in_specs=[whole(x.shape) for x in fixed] + [columns_of(x.shape[0]) for x in streamed],
-        out_specs=[whole(o.shape) for o in outs],
         out_shape=outs,
         scratch_shapes=[pltpu.VMEM((NLOAD, ORDER), BF16)],
         compiler_params=pltpu.CompilerParams(vmem_limit_bytes=VMEM_BYTES),
         cost_estimate=pl.CostEstimate(
             flops=2 * NLOAD * ORDER * ORDER, bytes_accessed=30 * 2**20, transcendentals=0
         ),
-    )(*fixed, *streamed)
+    )(*operands)
 
 
 def shards(
@@ -485,7 +460,7 @@
         chosen = [(a, b) for a, b in pairs if a % 2 == odd]
         return chosen + [(b, a) for a, b in chosen]
 
-    def exchange(xa, xb, ya, yb, xc):
+    def exchange(xc, xb, xa, yb, ya):
         rc = lax.ppermute(xc, "grp", across)
         ra = lax.ppermute(xa, "sub", swaps(sub_pairs, 0))
         rb = lax.ppermute(xb, "sub", swaps(sub_pairs, 1))
@@ -524,15 +499,15 @@
     field = sds((NLOAD, ORDER))
     small = sds((8, 128))
     ready = sds((count, 8, 128))
-    buffers = [sds((NLOAD, FACE))] * 4 + [sds((NLOAD, CONT))]
+    buffers = [sds((NLOAD, CONT))] + [sds((NLOAD, FACE))] * 4
 
     o_s, o_g, o_c, basis, coeff, act, code_columns, code_rows, *faces = call(
         prepare_kernel,
         [sds((FACE, FACE), BF16)] * 2
         + [sds((CONT, CONT), BF16), sds((8, ORDER)), small, sds((NLOAD, CONT))]
         + [sds((NLOAD, 128)), small]
-        + [sds((32, FACE))] * 4
-        + [sds((48, CONT))],
+        + [sds((48, CONT))]
+        + [sds((32, FACE))] * 4,
         coarse_basis[0], vp, coarse_coeff[0], face_order[0], partner, active_flags[0], step_codes, par,
     )
     t_stack, vh, vl, bh, bl, point, msg = call(
@@ -541,16 +516,15 @@
         + [sds((48, count * 8), BF16)] * 2
         + [sds((ORDER, 128), BF16)] * 2
         + [field, ready],
-        basis, vp, coeff, par, columns, *exchange(*faces),
+        basis, vp, coeff, par, columns, schur_block, dual_load[0], *exchange(*faces),
     )
     orders = (o_s, o_g, o_c)
 
     got = gathered(msg)
-    gh, gl, z, *faces = call_columns(
+    gh, gl, z, *faces = call_product(
         first_search_kernel,
         [sds((16, count * 8), BF16)] * 2 + [field] + buffers,
-        (got, vh, vl, par, point, t_stack) + orders,
-        (dual_load[0], schur_block),
+        got, vh, vl, par, point, t_stack, *orders, dual_load[0], schur_block,
     )
     image, msg = call(first_image_kernel, [field, ready], z, *exchange(*faces), par, bh, bl)
     got = gathered(msg)
@@ -564,11 +538,10 @@
     coef_q = jnp.zeros((56, 128), F32)
     for k in range(ITERS):
         got = gathered(msg)
-        coef_u, coef_q, scal, q, z, *faces = call_columns(
+        coef_u, coef_q, scal, q, z, *faces = call_product(
             functools.partial(search_kernel, k),
             [sds((56, 128))] * 2 + [small, field, field] + buffers,
-            (got, vh, vl, gh, gl, code_rows, scal, coef_q, par, u, q, t_stack) + orders,
-            (schur_block,),
+            got, vh, vl, gh, gl, code_rows, scal, coef_q, par, u, q, t_stack, *orders, schur_block,
         )
         image, msg = call(
             image_kernel,

time: 274 us -> 265 us (0.967)
  Pallas kernels: 42.2 us -> 33.3 us
    pallas_call x4, Pallas kernels: 25.9 us -> 17 us  [call_product(): pl.pallas_call(kernel, out_shape=outs, scratch_shapes=[pltpu.VMEM((NLOAD,...]
    unnamed x19 -> x13, local copies, waits for them, and re-layouts: 9.82 us -> 9.8 us
where the time goes in v3:
time: 265 us
  blocking collectives  171 us (65%)
  Pallas kernels  33.3 us (13%)
  starting transfers between devices  24.5 us (9%)
  waiting for transfers between devices  22.9 us (9%)
  local copies, waits for them, and re-layouts  11.7 us (4%)
    all_to_all x8, blocking collectives, gathered(): return lax.all_to_all(rows, AXES, 0, 0).reshape(count * 8, 128)  171 us
    ppermute x5, waiting for transfers between devices, exchange(): rc = lax.ppermute(xc, 'grp', across)  22.8 us
    pallas_call x4, Pallas kernels, call_product(): pl.pallas_call(kernel, out_shape=outs, scratch_shapes=[pltpu.VMEM((NLOAD,...  17 us
    pallas_call x10, Pallas kernels, call(): pl.pallas_call(kernel, out_shape=outs, compiler_params=pltpu.CompilerPara...  16.3 us
    unnamed x13, local copies, waits for them, and re-layouts  9.8 us
    ppermute x5, starting transfers between devices, exchange(): sa = lax.ppermute(ya, 'grp', swaps(grp_pairs, 0))  7.13 us
    ppermute x5, starting transfers between devices, exchange(): rc = lax.ppermute(xc, 'grp', across)  6.78 us
  transfers between devices with their start and end apart: 25, of which 5 were waited for; matrix products, arithmetic and copies ran while one was open for 0% of the time, Pallas kernels for 0%

profile of v3, /device:TPU:1, one launch (start us, length us, event | category | flops | bytes accessed | tf_op | source)
XLA Modules:
  0.0 264.5 jit_solution(5652340838264433267)
XLA Ops:
  0.7 0.7 copy.21
  1.4 0.8 copy.12.codes
  2.2 0.8 copy.20
  3.0 1.1 reshape.34
  4.6 0.9 copy-done.3
  5.4 0.7 copy-done.4
  6.1 1.1 shard_map.104
  7.3 2.1 collective-permute-start
  10.1 1.0 collective-permute-start.2
  11.7 4.3 %collective-permute-start.4 = (f32[48,256]{1,0:T(8,128)S(1)}, f32[48,256]{1,0:T(8,128)S(1)}, u32[]{:S(2)}, u32[]{:S(2)}) collective-permute-start(f32[48,256]{1,0:T(8,128)S(1)} %get-tuple-element.89), channel_id=1, source_target_pairs={{0,4},{1,5},{2,6},{3,7},{4,0},{5,1},{6,2},{7,3},{8,12},{9,13},{10,... | collective-permute-start | bytes 147464 | tf_op jit(solution)/shard_map/ppermute | solution.py:464
  16.5 1.0 collective-permute-done.4.rc
  17.6 4.7 %copy-done = bf16[1,2560,2560]{2,1,0:T(8,128)(2,1)S(1)} copy-done((bf16[1,2560,2560]{2,1,0:T(8,128)(2,1)S(1)}, bf16[1,2560,2560]{2,1,0:T(8,128)(2,1)}, u32[]{:S(2)}) %copy-start) | copy-done | bytes 13107224
  22.3 1.2 copy-done.2
  23.5 1.8 shard_map.105
  25.3 27.2 %all_to_all.40 = f32[128,8,128]{2,1,0:T(8,128)S(1)} all-to-all(f32[128,8,128]{2,1,0:T(8,128)S(1)} %get-tuple-element.90), channel_id=1, replica_groups=mesh['sub'=16,'grp'=8] {'sub','grp'}, dimensions={0} | all-to-all | bytes 1048576 | tf_op jit(solution)/shard_map/all_to_all | solution.py:472
  52.5 4.2 %shard_map.106 = (bf16[16,1024]{1,0:T(8,128)(2,1)S(1)}, bf16[16,1024]{1,0:T(8,128)(2,1)S(1)}, f32[96,2560]{1,0:T(8,128)S(1)}, f32[96,256]{1,0:T(8,128)S(1)}, f32...) custom-call(f32[1024,128]{1,0:T(8,128)S(1)} %bitcast.37, ...), custom_call_target="tpu_custom_call" | custom-call | flops 1258291200 | bytes 31457280 | tf_op jit(solution)/shard_map/pallas_call | solution.py:429
  57.2 0.7 collective-permute-start.6
  57.8 1.5 collective-permute-start.7
  59.4 0.7 collective-permute-start.8
  60.6 5.4 %collective-permute-done.9.rc = f32[96,256]{1,0:T(8,128)S(1)} collective-permute-done((f32[96,256]{1,0:T(8,128)S(1)}, f32[96,256]{1,0:T(8,128)S(1)}, u32[]{:S(2)}, u32[]{:S(2)}) %collective-permute-start.9) | collective-permute-done | bytes 98336 | tf_op jit(solution)/shard_map/ppermute | solution.py:464
  66.7 22.5 %all_to_all.41 = f32[128,8,128]{2,1,0:T(8,128)S(1)} all-to-all(f32[128,8,128]{2,1,0:T(8,128)S(1)} %get-tuple-element.106), channel_id=1, replica_groups=mesh['sub'=16,'grp'=8] {'sub','grp'}, dimensions={0} | all-to-all | bytes 1048576 | tf_op jit(solution)/shard_map/all_to_all | solution.py:472
  89.2 2.0 shard_map.108
  91.3 17.9 %all_to_all.42 = f32[128,8,128]{2,1,0:T(8,128)S(1)} all-to-all(f32[128,8,128]{2,1,0:T(8,128)S(1)} %get-tuple-element.110), channel_id=1, replica_groups=mesh['sub'=16,'grp'=8] {'sub','grp'}, dimensions={0} | all-to-all | bytes 1048576 | tf_op jit(solution)/shard_map/all_to_all | solution.py:472
  109.2 4.2 %shard_map.109 = (f32[56,128]{1,0:T(8,128)S(1)}, f32[56,128]{1,0:T(8,128)S(1)}, f32[8,128]{1,0:T(8,128)S(1)}, f32[96,2560]{1,0:T(8,128)S(1)}, f32[96,2560]{1,0:T...) custom-call(f32[1024,128]{1,0:T(8,128)S(1)} %bitcast.30, ...), custom_call_target="tpu_custom_call" | custom-call | flops 1258291200 | bytes 31457280 | tf_op jit(solution)/shard_map/pallas_call | solution.py:429
  113.9 0.7 collective-permute-start.11
  114.6 1.5 collective-permute-start.12
  116.1 0.7 collective-permute-start.13
  117.3 5.4 %collective-permute-done.14.rc = f32[96,256]{1,0:T(8,128)S(1)} collective-permute-done((f32[96,256]{1,0:T(8,128)S(1)}, f32[96,256]{1,0:T(8,128)S(1)}, u32[]{:S(2)}, u32[]{:S(2)}) %collective-permute-start.14) | collective-permute-done | bytes 98336 | tf_op jit(solution)/shard_map/ppermute | solution.py:464
  122.8 1.0 shard_map.110
  123.8 22.5 %all_to_all.43 = f32[128,8,128]{2,1,0:T(8,128)S(1)} all-to-all(f32[128,8,128]{2,1,0:T(8,128)S(1)} %get-tuple-element.124), channel_id=1, replica_groups=mesh['sub'=16,'grp'=8] {'sub','grp'}, dimensions={0} | all-to-all | bytes 1048576 | tf_op jit(solution)/shard_map/all_to_all | solution.py:472
  146.3 2.3 shard_map.111
  148.7 17.9 %all_to_all.44 = f32[128,8,128]{2,1,0:T(8,128)S(1)} all-to-all(f32[128,8,128]{2,1,0:T(8,128)S(1)} %get-tuple-element.128), channel_id=1, replica_groups=mesh['sub'=16,'grp'=8] {'sub','grp'}, dimensions={0} | all-to-all | bytes 1048576 | tf_op jit(solution)/shard_map/all_to_all | solution.py:472
  166.6 4.3 %shard_map.112 = (f32[56,128]{1,0:T(8,128)S(1)}, f32[56,128]{1,0:T(8,128)S(1)}, f32[8,128]{1,0:T(8,128)S(1)}, f32[96,2560]{1,0:T(8,128)S(1)}, f32[96,2560]{1,0:T...) custom-call(f32[1024,128]{1,0:T(8,128)S(1)} %bitcast.33, ...), custom_call_target="tpu_custom_call" | custom-call | flops 1258291200 | bytes 31457280 | tf_op jit(solution)/shard_map/pallas_call | solution.py:429
  171.3 0.7 collective-permute-start.16
  172.0 1.5 collective-permute-start.17
  174.8 5.4 %collective-permute-done.19.rc = f32[96,256]{1,0:T(8,128)S(1)} collective-permute-done((f32[96,256]{1,0:T(8,128)S(1)}, f32[96,256]{1,0:T(8,128)S(1)}, u32[]{:S(2)}, u32[]{:S(2)}) %collective-permute-start.19) | collective-permute-done | bytes 98336 | tf_op jit(solution)/shard_map/ppermute | solution.py:464
  180.2 1.0 shard_map.113
  181.2 22.5 %all_to_all.45 = f32[128,8,128]{2,1,0:T(8,128)S(1)} all-to-all(f32[128,8,128]{2,1,0:T(8,128)S(1)} %get-tuple-element.140), channel_id=1, replica_groups=mesh['sub'=16,'grp'=8] {'sub','grp'}, dimensions={0} | all-to-all | bytes 1048576 | tf_op jit(solution)/shard_map/all_to_all | solution.py:472
  203.7 2.4 shard_map.114
  206.1 17.9 %all_to_all.46 = f32[128,8,128]{2,1,0:T(8,128)S(1)} all-to-all(f32[128,8,128]{2,1,0:T(8,128)S(1)} %get-tuple-element.145), channel_id=1, replica_groups=mesh['sub'=16,'grp'=8] {'sub','grp'}, dimensions={0} | all-to-all | bytes 1048576 | tf_op jit(solution)/shard_map/all_to_all | solution.py:472
  224.0 4.3 %shard_map.115 = (f32[56,128]{1,0:T(8,128)S(1)}, f32[56,128]{1,0:T(8,128)S(1)}, f32[8,128]{1,0:T(8,128)S(1)}, f32[96,2560]{1,0:T(8,128)S(1)}, f32[96,2560]{1,0:T...) custom-call(f32[1024,128]{1,0:T(8,128)S(1)} %bitcast.31, ...), custom_call_target="tpu_custom_call" | custom-call | flops 1258291200 | bytes 31457280 | tf_op jit(solution)/shard_map/pallas_call | solution.py:429
  228.8 0.7 collective-permute-start.21
  229.4 1.5 collective-permute-start.22
  231.6 0.8 collective-permute-start.24
  232.4 5.4 %collective-permute-done.24.rc = f32[96,256]{1,0:T(8,128)S(1)} collective-permute-done((f32[96,256]{1,0:T(8,128)S(1)}, f32[96,256]{1,0:T(8,128)S(1)}, u32[]{:S(2)}, u32[]{:S(2)}) %collective-permute-start.24) | collective-permute-done | bytes 98336 | tf_op jit(solution)/shard_map/ppermute | solution.py:464
  237.9 0.9 shard_map.116
  238.8 22.5 %all_to_all.47 = f32[128,8,128]{2,1,0:T(8,128)S(1)} all-to-all(f32[128,8,128]{2,1,0:T(8,128)S(1)} %get-tuple-element.157), channel_id=1, replica_groups=mesh['sub'=16,'grp'=8] {'sub','grp'}, dimensions={0} | all-to-all | bytes 1048576 | tf_op jit(solution)/shard_map/all_to_all | solution.py:472
  261.4 3.2 %shard_map.117 = (f32[96,2560]{1,0:T(8,128)}, f32[96,2560]{1,0:T(8,128)}) custom-call(f32[1024,128]{1,0:T(8,128)S(1)} %bitcast.35, bf16[48,1024]{1,0:T(8,128)(2,1)S(1)} %get-tuple-element.91.vh, bf16[48,1024]{1,0:T(8,128)(2,1)S(1)} %get-tuple-element.92.vl, f32[8,128]{1,0:T(8,128)S(1)} %get-tuple-element.113.codes.codes_rows, ...), custom_call_target="tpu_custom_call" | custom-call | bytes 9117696 | tf_op jit(solution)/shard_map/pallas_call | solution.py:420
  (53 shorter events, 7.7 us)
Async XLA Ops:
  4.5 0.9 copy-start.3
  5.4 0.7 copy-start.4
  7.3 10.3 %collective-permute-start = (f32[32,512]{1,0:T(8,128)S(1)}, f32[32,512]{1,0:T(8,128)S(1)}, u32[]{:S(2)}, u32[]{:S(2)}) collective-permute-start(f32[32,512]{1,0:T(8,128)S(1)} %get-tuple-element.85), channel_id=1, source_target_pairs={{0,8},{16,24},{32,40},{48,56},{64,72},{80,88},{96,104},{112,120},{... | collective-permute-start | bytes 196616 | tf_op jit(solution)/shard_map/ppermute | solution.py:465
  9.4 8.2 %collective-permute-start.1 = (f32[32,512]{1,0:T(8,128)S(1)}, f32[32,512]{1,0:T(8,128)S(1)}, u32[]{:S(2)}, u32[]{:S(2)}) collective-permute-start(f32[32,512]{1,0:T(8,128)S(1)} %get-tuple-element.86), channel_id=1, source_target_pairs={{8,16},{24,32},{40,48},{56,64},{72,80},{88,96},{104,112},{16,8},{3... | collective-permute-start | bytes 196616 | tf_op jit(solution)/shard_map/ppermute | solution.py:466
  10.1 7.5 %collective-permute-start.2 = (f32[32,512]{1,0:T(8,128)S(1)}, f32[32,512]{1,0:T(8,128)S(1)}, u32[]{:S(2)}, u32[]{:S(2)}) collective-permute-start(f32[32,512]{1,0:T(8,128)S(1)} %get-tuple-element.87), channel_id=1, source_target_pairs={{0,1},{2,3},{4,5},{6,7},{1,0},{3,2},{5,4},{7,6},{8,9},{10,11},{12,... | collective-permute-start | bytes 196616 | tf_op jit(solution)/shard_map/ppermute | solution.py:468
  11.1 6.5 %collective-permute-start.3 = (f32[32,512]{1,0:T(8,128)S(1)}, f32[32,512]{1,0:T(8,128)S(1)}, u32[]{:S(2)}, u32[]{:S(2)}) collective-permute-start(f32[32,512]{1,0:T(8,128)S(1)} %get-tuple-element.88), channel_id=1, source_target_pairs={{3,4},{4,3},{11,12},{12,11},{19,20},{20,19},{27,28},{28,27},{35,36... | collective-permute-start | bytes 196616 | tf_op jit(solution)/shard_map/ppermute | solution.py:467
  11.7 5.8 %collective-permute-start.4 = (f32[48,256]{1,0:T(8,128)S(1)}, f32[48,256]{1,0:T(8,128)S(1)}, u32[]{:S(2)}, u32[]{:S(2)}) collective-permute-start(f32[48,256]{1,0:T(8,128)S(1)} %get-tuple-element.89), channel_id=1, source_target_pairs={{0,4},{1,5},{2,6},{3,7},{4,0},{5,1},{6,2},{7,3},{8,12},{9,13},{10,... | collective-permute-start | bytes 147464 | tf_op jit(solution)/shard_map/ppermute | solution.py:464
  17.6 4.7 %copy-start = (bf16[1,2560,2560]{2,1,0:T(8,128)(2,1)S(1)}, bf16[1,2560,2560]{2,1,0:T(8,128)(2,1)}, u32[]{:S(2)}) copy-start(bf16[1,2560,2560]{2,1,0:T(8,128)(2,1)} %param.9) | copy-start | bytes 39321604
  22.3 1.2 copy-start.2
  23.5 29.0 %copy-start.1 = (bf16[1,2560,2560]{2,1,0:T(8,128)(2,1)S(1)}, bf16[1,2560,2560]{2,1,0:T(8,128)(2,1)}, u32[]{:S(2)}) copy-start(bf16[1,2560,2560]{2,1,0:T(8,128)(2,1)} %param.9) | copy-start | bytes 39321604
  56.7 9.3 %collective-permute-start.5 = (f32[96,512]{1,0:T(8,128)S(1)}, f32[96,512]{1,0:T(8,128)S(1)}, u32[]{:S(2)}, u32[]{:S(2)}) collective-permute-start(f32[96,512]{1,0:T(8,128)S(1)} %get-tuple-element.99), channel_id=1, source_target_pairs={{0,8},{16,24},{32,40},{48,56},{64,72},{80,88},{96,104},{112,120},{... | collective-permute-start | bytes 589832 | tf_op jit(solution)/shard_map/ppermute | solution.py:465
  57.2 8.9 %collective-permute-start.6 = (f32[96,512]{1,0:T(8,128)S(1)}, f32[96,512]{1,0:T(8,128)S(1)}, u32[]{:S(2)}, u32[]{:S(2)}) collective-permute-start(f32[96,512]{1,0:T(8,128)S(1)} %get-tuple-element.100), channel_id=1, source_target_pairs={{8,16},{24,32},{40,48},{56,64},{72,80},{88,96},{104,112},{16,8},{3... | collective-permute-start | bytes 589832 | tf_op jit(solution)/shard_map/ppermute | solution.py:466
  57.8 8.2 %collective-permute-start.7 = (f32[96,512]{1,0:T(8,128)S(1)}, f32[96,512]{1,0:T(8,128)S(1)}, u32[]{:S(2)}, u32[]{:S(2)}) collective-permute-start(f32[96,512]{1,0:T(8,128)S(1)} %get-tuple-element.101), channel_id=1, source_target_pairs={{0,1},{2,3},{4,5},{6,7},{1,0},{3,2},{5,4},{7,6},{8,9},{10,11},{12,... | collective-permute-start | bytes 589832 | tf_op jit(solution)/shard_map/ppermute | solution.py:468
  59.4 6.7 %collective-permute-start.8 = (f32[96,512]{1,0:T(8,128)S(1)}, f32[96,512]{1,0:T(8,128)S(1)}, u32[]{:S(2)}, u32[]{:S(2)}) collective-permute-start(f32[96,512]{1,0:T(8,128)S(1)} %get-tuple-element.102), channel_id=1, source_target_pairs={{3,4},{4,3},{11,12},{12,11},{19,20},{20,19},{27,28},{28,27},{35,36... | collective-permute-start | bytes 589832 | tf_op jit(solution)/shard_map/ppermute | solution.py:467
  60.0 6.0 %collective-permute-start.9 = (f32[96,256]{1,0:T(8,128)S(1)}, f32[96,256]{1,0:T(8,128)S(1)}, u32[]{:S(2)}, u32[]{:S(2)}) collective-permute-start(f32[96,256]{1,0:T(8,128)S(1)} %get-tuple-element.103), channel_id=1, source_target_pairs={{0,4},{1,5},{2,6},{3,7},{4,0},{5,1},{6,2},{7,3},{8,12},{9,13},{10,... | collective-permute-start | bytes 294920 | tf_op jit(solution)/shard_map/ppermute | solution.py:464
  113.5 9.3 %collective-permute-start.10 = (f32[96,512]{1,0:T(8,128)S(1)}, f32[96,512]{1,0:T(8,128)S(1)}, u32[]{:S(2)}, u32[]{:S(2)}) collective-permute-start(f32[96,512]{1,0:T(8,128)S(1)} %get-tuple-element.116), channel_id=1, source_target_pairs={{0,8},{16,24},{32,40},{48,56},{64,72},{80,88},{96,104},{112,120},{... | collective-permute-start | bytes 589832 | tf_op jit(solution)/shard_map/ppermute | solution.py:465
  113.9 8.9 %collective-permute-start.11 = (f32[96,512]{1,0:T(8,128)S(1)}, f32[96,512]{1,0:T(8,128)S(1)}, u32[]{:S(2)}, u32[]{:S(2)}) collective-permute-start(f32[96,512]{1,0:T(8,128)S(1)} %get-tuple-element.117), channel_id=1, source_target_pairs={{8,16},{24,32},{40,48},{56,64},{72,80},{88,96},{104,112},{16,8},{3... | collective-permute-start | bytes 589832 | tf_op jit(solution)/shard_map/ppermute | solution.py:466
  114.6 8.2 %collective-permute-start.12 = (f32[96,512]{1,0:T(8,128)S(1)}, f32[96,512]{1,0:T(8,128)S(1)}, u32[]{:S(2)}, u32[]{:S(2)}) collective-permute-start(f32[96,512]{1,0:T(8,128)S(1)} %get-tuple-element.118), channel_id=1, source_target_pairs={{0,1},{2,3},{4,5},{6,7},{1,0},{3,2},{5,4},{7,6},{8,9},{10,11},{12,... | collective-permute-start | bytes 589832 | tf_op jit(solution)/shard_map/ppermute | solution.py:468
  116.1 6.7 %collective-permute-start.13 = (f32[96,512]{1,0:T(8,128)S(1)}, f32[96,512]{1,0:T(8,128)S(1)}, u32[]{:S(2)}, u32[]{:S(2)}) collective-permute-start(f32[96,512]{1,0:T(8,128)S(1)} %get-tuple-element.119), channel_id=1, source_target_pairs={{3,4},{4,3},{11,12},{12,11},{19,20},{20,19},{27,28},{28,27},{35,36... | collective-permute-start | bytes 589832 | tf_op jit(solution)/shard_map/ppermute | solution.py:467
  116.8 6.0 %collective-permute-start.14 = (f32[96,256]{1,0:T(8,128)S(1)}, f32[96,256]{1,0:T(8,128)S(1)}, u32[]{:S(2)}, u32[]{:S(2)}) collective-permute-start(f32[96,256]{1,0:T(8,128)S(1)} %get-tuple-element.120), channel_id=1, source_target_pairs={{0,4},{1,5},{2,6},{3,7},{4,0},{5,1},{6,2},{7,3},{8,12},{9,13},{10,... | collective-permute-start | bytes 294920 | tf_op jit(solution)/shard_map/ppermute | solution.py:464
  170.9 9.3 %collective-permute-start.15 = (f32[96,512]{1,0:T(8,128)S(1)}, f32[96,512]{1,0:T(8,128)S(1)}, u32[]{:S(2)}, u32[]{:S(2)}) collective-permute-start(f32[96,512]{1,0:T(8,128)S(1)} %get-tuple-element.132), channel_id=1, source_target_pairs={{0,8},{16,24},{32,40},{48,56},{64,72},{80,88},{96,104},{112,120},{... | collective-permute-start | bytes 589832 | tf_op jit(solution)/shard_map/ppermute | solution.py:465
  171.3 8.9 %collective-permute-start.16 = (f32[96,512]{1,0:T(8,128)S(1)}, f32[96,512]{1,0:T(8,128)S(1)}, u32[]{:S(2)}, u32[]{:S(2)}) collective-permute-start(f32[96,512]{1,0:T(8,128)S(1)} %get-tuple-element.133), channel_id=1, source_target_pairs={{8,16},{24,32},{40,48},{56,64},{72,80},{88,96},{104,112},{16,8},{3... | collective-permute-start | bytes 589832 | tf_op jit(solution)/shard_map/ppermute | solution.py:466
  172.0 8.2 %collective-permute-start.17 = (f32[96,512]{1,0:T(8,128)S(1)}, f32[96,512]{1,0:T(8,128)S(1)}, u32[]{:S(2)}, u32[]{:S(2)}) collective-permute-start(f32[96,512]{1,0:T(8,128)S(1)} %get-tuple-element.134), channel_id=1, source_target_pairs={{0,1},{2,3},{4,5},{6,7},{1,0},{3,2},{5,4},{7,6},{8,9},{10,11},{12,... | collective-permute-start | bytes 589832 | tf_op jit(solution)/shard_map/ppermute | solution.py:468
  173.5 6.7 %collective-permute-start.18 = (f32[96,512]{1,0:T(8,128)S(1)}, f32[96,512]{1,0:T(8,128)S(1)}, u32[]{:S(2)}, u32[]{:S(2)}) collective-permute-start(f32[96,512]{1,0:T(8,128)S(1)} %get-tuple-element.135), channel_id=1, source_target_pairs={{3,4},{4,3},{11,12},{12,11},{19,20},{20,19},{27,28},{28,27},{35,36... | collective-permute-start | bytes 589832 | tf_op jit(solution)/shard_map/ppermute | solution.py:467
  174.2 6.0 %collective-permute-start.19 = (f32[96,256]{1,0:T(8,128)S(1)}, f32[96,256]{1,0:T(8,128)S(1)}, u32[]{:S(2)}, u32[]{:S(2)}) collective-permute-start(f32[96,256]{1,0:T(8,128)S(1)} %get-tuple-element.136), channel_id=1, source_target_pairs={{0,4},{1,5},{2,6},{3,7},{4,0},{5,1},{6,2},{7,3},{8,12},{9,13},{10,... | collective-permute-start | bytes 294920 | tf_op jit(solution)/shard_map/ppermute | solution.py:464
  228.3 9.6 %collective-permute-start.20 = (f32[96,512]{1,0:T(8,128)S(1)}, f32[96,512]{1,0:T(8,128)S(1)}, u32[]{:S(2)}, u32[]{:S(2)}) collective-permute-start(f32[96,512]{1,0:T(8,128)S(1)} %get-tuple-element.149), channel_id=1, source_target_pairs={{0,8},{16,24},{32,40},{48,56},{64,72},{80,88},{96,104},{112,120},{... | collective-permute-start | bytes 589832 | tf_op jit(solution)/shard_map/ppermute | solution.py:465
  228.8 9.1 %collective-permute-start.21 = (f32[96,512]{1,0:T(8,128)S(1)}, f32[96,512]{1,0:T(8,128)S(1)}, u32[]{:S(2)}, u32[]{:S(2)}) collective-permute-start(f32[96,512]{1,0:T(8,128)S(1)} %get-tuple-element.150), channel_id=1, source_target_pairs={{8,16},{24,32},{40,48},{56,64},{72,80},{88,96},{104,112},{16,8},{3... | collective-permute-start | bytes 589832 | tf_op jit(solution)/shard_map/ppermute | solution.py:466
  229.4 8.5 %collective-permute-start.22 = (f32[96,512]{1,0:T(8,128)S(1)}, f32[96,512]{1,0:T(8,128)S(1)}, u32[]{:S(2)}, u32[]{:S(2)}) collective-permute-start(f32[96,512]{1,0:T(8,128)S(1)} %get-tuple-element.151), channel_id=1, source_target_pairs={{0,1},{2,3},{4,5},{6,7},{1,0},{3,2},{5,4},{7,6},{8,9},{10,11},{12,... | collective-permute-start | bytes 589832 | tf_op jit(solution)/shard_map/ppermute | solution.py:468
  231.0 6.9 %collective-permute-start.23 = (f32[96,512]{1,0:T(8,128)S(1)}, f32[96,512]{1,0:T(8,128)S(1)}, u32[]{:S(2)}, u32[]{:S(2)}) collective-permute-start(f32[96,512]{1,0:T(8,128)S(1)} %get-tuple-element.152), channel_id=1, source_target_pairs={{3,4},{4,3},{11,12},{12,11},{19,20},{20,19},{27,28},{28,27},{35,36... | collective-permute-start | bytes 589832 | tf_op jit(solution)/shard_map/ppermute | solution.py:467
  231.6 6.2 %collective-permute-start.24 = (f32[96,256]{1,0:T(8,128)S(1)}, f32[96,256]{1,0:T(8,128)S(1)}, u32[]{:S(2)}, u32[]{:S(2)}) collective-permute-start(f32[96,256]{1,0:T(8,128)S(1)} %get-tuple-element.153), channel_id=1, source_target_pairs={{0,4},{1,5},{2,6},{3,7},{4,0},{5,1},{6,2},{7,3},{8,12},{9,13},{10,... | collective-permute-start | bytes 294920 | tf_op jit(solution)/shard_map/ppermute | solution.py:464
